TPU v7x, 512 devices: a whole 4x4x16 slice. The times are simulated.
512 devices in a mesh: dp: 8 (over x, core), ctx: 16 (over z), tp: 4 (over y).
Axes of the slice: x: 4, y: 4, z: 16, core: 2. Of those that a mesh axis runs over, the one named last changes fastest.
Arguments:
- tokens: bfloat16 [2048, 4096], P('ctx', ('dp', 'tp')), may hold values from -6 to 6
- expert_ids: int32 [2048, 8], P(('ctx', 'tp')), may hold values from 0 to 63, all different within a row; in each aligned block of 32 rows (0 to 31, 32 to 63, ...) at most 6 rows name the same one
- gate_codes: int32 [2048, 8], P(('ctx', 'tp')), may hold values from 16 to 255
- gate_weight: bfloat16 [64, 4096, 768], P(('ctx', 'tp'), 'dp'), may hold values from -0.09375 to 0.09375
- up_weight: bfloat16 [64, 4096, 768], P(('ctx', 'tp'), 'dp'), may hold values from -0.09375 to 0.09375
- down_weight: bfloat16 [64, 4096, 768], P(('ctx', 'tp'), 'dp'), may hold values from -0.21875 to 0.21875
- out_grad: bfloat16 [2048, 4096], P('ctx', ('dp', 'tp')), may hold values from -1.5 to 1.5
Outputs:
- layer_out: bfloat16 [2048, 4096], P(('ctx', 'tp'), 'dp')
- token_grad: bfloat16 [2048, 4096], P(('ctx', 'tp'), 'dp')
- gate_grad: bfloat16 [64, 4096, 768], P(('ctx', 'tp'), 'dp')
- up_grad: bfloat16 [64, 4096, 768], P(('ctx', 'tp'), 'dp')
- down_grad: bfloat16 [64, 4096, 768], P(('ctx', 'tp'), 'dp')
Inputs may be any that keep to these rules, and one draw needn't show every extreme that they name: `expert_ids`: each row names 8 different experts. In each aligned block of 32 rows (the rows of one device of ctx+tp) no expert is named by more than 6 rows, and in some block an expert is named by exactly 6.
All inputs are finite; a program needn't handle non-finite values.
Results may differ from a plain program's by a relative error of at most 0.0064.
Values may be sent and summed in bfloat16 or wider, within the bound.
A program may use at most 64 MiB of HBM per device.

v0:
```python
import jax
import jax.numpy as jnp
from jax import lax
from jax.sharding import PartitionSpec as P


def send_out(payload, n_ctx, n_tp):
    shaped = tuple((part.reshape(n_ctx * n_tp, -1, part.shape[-1]) for part in payload))
    moved = (
        lax.all_to_all(shaped[0], ("ctx", "tp"), split_axis=0, concat_axis=0, tiled=True),
        lax.all_to_all(shaped[1], ("ctx", "tp"), split_axis=0, concat_axis=0, tiled=True),
    )
    return tuple((part.reshape(-1, part.shape[-1]) for part in moved))


def send_back(payload, n_ctx, n_tp):
    shaped = payload.reshape(n_ctx * n_tp, -1, payload.shape[-1])
    moved = lax.all_to_all(shaped, ("ctx", "tp"), split_axis=0, concat_axis=0, tiled=True)
    return moved.reshape(-1, payload.shape[-1])


def contract_first(left, right):
    return lax.dot_general(
        left, right, (((0,), (0,)), ((), ())), preferred_element_type=jnp.float32
    )


def contract_last(left, right):
    return lax.dot_general(
        left, right, (((1,), (1,)), ((), ())), preferred_element_type=jnp.float32
    )


def shards(tokens, expert_ids, gate_codes, gate_weight, up_weight, down_weight, out_grad):
    n_ctx = lax.axis_size("ctx")
    n_tp = lax.axis_size("tp")
    experts = n_ctx * n_tp
    tok_fold, top_count = expert_ids.shape
    capacity = max(2, 3 * tok_fold * top_count // (2 * experts))
    fold_rows, fold_grads = (
        lax.all_to_all(tokens, "tp", split_axis=0, concat_axis=1, tiled=True),
        lax.all_to_all(out_grad, "tp", split_axis=0, concat_axis=1, tiled=True),
    )
    flat_ids = expert_ids.reshape(-1)
    count_all = flat_ids.shape[0]
    owners = (flat_ids[:, None] == jnp.arange(experts, dtype=jnp.int32)[None, :]).astype(
        jnp.bfloat16
    )
    positions = jnp.arange(count_all, dtype=jnp.int32)
    earlier = (positions[:, None] >= positions[None, :]).astype(jnp.bfloat16)
    running = jnp.dot(earlier, owners, preferred_element_type=jnp.float32)
    slot_index = jnp.sum(running * owners.astype(jnp.float32), axis=1).astype(jnp.int32) - 1
    target = (flat_ids * capacity + slot_index).reshape(tok_fold, top_count)
    places = jnp.arange(experts * capacity, dtype=jnp.int32)
    chosen = places[:, None, None] == target[None, :, :]
    gate_values = gate_codes.astype(jnp.float32) / 256.0
    picker = jnp.sum(chosen.astype(jnp.float32), axis=2).astype(jnp.bfloat16)
    gated_pick = jnp.sum(jnp.where(chosen, gate_values[None, :, :], 0.0), axis=2).astype(
        jnp.bfloat16
    )
    send_rows = jnp.dot(picker, fold_rows, preferred_element_type=jnp.float32).astype(jnp.bfloat16)
    send_grads = jnp.dot(gated_pick, fold_grads, preferred_element_type=jnp.float32).astype(
        jnp.bfloat16
    )
    expert_rows, slot_grad = send_out((send_rows, send_grads), n_ctx, n_tp)
    gate_w = gate_weight[0]
    up_w = up_weight[0]
    down_w = down_weight[0]
    part_gate = jnp.dot(expert_rows, gate_w, preferred_element_type=jnp.float32)
    part_up = jnp.dot(expert_rows, up_w, preferred_element_type=jnp.float32)
    part_hidden = jnp.dot(slot_grad, down_w, preferred_element_type=jnp.float32)
    pre_gate, pre_up = lax.psum((part_gate, part_up), "dp")
    squash = jax.nn.sigmoid(pre_gate)
    hidden = (pre_gate * squash * pre_up).astype(jnp.bfloat16)
    hidden_grad = lax.psum(part_hidden, "dp")
    gate_pre = (hidden_grad * pre_up * squash * (1.0 + pre_gate * (1.0 - squash))).astype(
        jnp.bfloat16
    )
    up_pre = (hidden_grad * pre_gate * squash).astype(jnp.bfloat16)
    expert_out = contract_last(hidden, down_w).astype(jnp.bfloat16)
    returned = send_back(expert_out, n_ctx, n_tp)
    layer_out = contract_first(gated_pick, returned).astype(jnp.bfloat16)
    row_grad = (contract_last(gate_pre, gate_w) + contract_last(up_pre, up_w)).astype(jnp.bfloat16)
    returned_grad = send_back(row_grad, n_ctx, n_tp)
    token_grad = contract_first(picker, returned_grad).astype(jnp.bfloat16)
    gate_grad = contract_first(expert_rows, gate_pre).astype(jnp.bfloat16)
    up_grad = contract_first(expert_rows, up_pre).astype(jnp.bfloat16)
    down_grad = contract_first(slot_grad, hidden).astype(jnp.bfloat16)
    return (layer_out, token_grad, gate_grad[None], up_grad[None], down_grad[None])


def solution(mesh):
    placed = (
        P("ctx", ("dp", "tp")),
        P(("ctx", "tp"), None),
        P(("ctx", "tp"), None),
        P(("ctx", "tp"), "dp", None),
        P(("ctx", "tp"), "dp", None),
        P(("ctx", "tp"), "dp", None),
        P("ctx", ("dp", "tp")),
    )
    return jax.shard_map(
        shards,
        mesh=mesh,
        in_specs=placed,
        out_specs=(
            P(("ctx", "tp"), "dp"),
            P(("ctx", "tp"), "dp"),
            P(("ctx", "tp"), "dp", None),
            P(("ctx", "tp"), "dp", None),
            P(("ctx", "tp"), "dp", None),
        ),
        check_vma=False,
    )
```

profile of v0, /device:TPU:6, one launch (start us, length us, event | category | flops | bytes accessed | tf_op | source)
XLA Modules:
  0.0 291.6 jit_solution(8671093586838972735)
XLA Ops:
  7.2 0.0 copy-start
  7.2 4.6 %all-to-all-start = ((bf16[4,32,128]{2,1,0:T(8,128)(2,1)}), bf16[4,32,128]{2,1,0:T(8,128)(2,1)S(1)}, u32[]{:S(2)}, u32[]{:S(2)}) async-start(bf16[4,32,128]{2,1,0:T(8,128)(2,1)} %bitcast.57), calls=%async_computation | async-start | bytes 65536 | tf_op jit(solution)/shard_map/all_to_all | solution.py:41
  11.8 0.7 convert_multiply_fusion
  12.5 0.1 copy.26
  12.6 0.8 copy.24
  13.3 0.1 eq.29
  13.4 0.2 fusion.4
  13.6 0.1 sub.10
  13.7 0.3 select_reduce_fusion
  14.1 3.2 %all-to-all-done = bf16[4,32,128]{2,1,0:T(8,128)(2,1)S(1)} async-done(((bf16[4,32,128]{2,1,0:T(8,128)(2,1)}), bf16[4,32,128]{2,1,0:T(8,128)(2,1)S(1)}, u32[]{:S(2)}, u32[]{:S(2)}) %all-to-all-start) | async-done | bytes 32800 | tf_op jit(solution)/shard_map/all_to_all | solution.py:41
  17.2 3.3 %all-to-all-start.3 = ((bf16[4,32,128]{2,1,0:T(8,128)(2,1)}), bf16[4,32,128]{2,1,0:T(8,128)(2,1)S(1)}, u32[]{:S(2)}, u32[]{:S(2)}) async-start(bf16[4,32,128]{2,1,0:T(8,128)(2,1)} %bitcast.58), calls=%async_computation.3 | async-start | bytes 65536 | tf_op jit(solution)/shard_map/all_to_all | solution.py:42
  20.5 0.3 convolution_convert_fusion.5
  20.8 0.9 reshape.54
  21.7 4.2 %all-to-all-done.3 = bf16[4,32,128]{2,1,0:T(8,128)(2,1)S(1)} async-done(((bf16[4,32,128]{2,1,0:T(8,128)(2,1)}), bf16[4,32,128]{2,1,0:T(8,128)(2,1)S(1)}, u32[]{:S(2)}, u32[]{:S(2)}) %all-to-all-start.3) | async-done | bytes 32800 | tf_op jit(solution)/shard_map/all_to_all | solution.py:42
  25.9 16.7 %all-to-all-start.1 = ((bf16[64,6,512]{2,1,0:T(8,128)(2,1)}), bf16[64,6,512]{2,1,0:T(8,128)(2,1)S(1)}, u32[]{:S(2)}, u32[]{:S(2)}) async-start(bf16[64,6,512]{2,1,0:T(8,128)(2,1)} %reshape.54), calls=%async_computation.1 | async-start | bytes 1048576 | tf_op jit(solution)/shard_map/all_to_all | solution.py:10
  42.7 0.3 convolution_convert_fusion.3
  42.9 0.9 reshape.58
  43.9 29.0 %all-to-all-done.1 = bf16[64,6,512]{2,1,0:T(8,128)(2,1)S(1)} async-done(((bf16[64,6,512]{2,1,0:T(8,128)(2,1)}), bf16[64,6,512]{2,1,0:T(8,128)(2,1)S(1)}, u32[]{:S(2)}, u32[]{:S(2)}) %all-to-all-start.1) | async-done | bytes 393248 | tf_op jit(solution)/shard_map/all_to_all | solution.py:10
  72.9 6.1 %all-to-all-start.4 = ((bf16[64,6,512]{2,1,0:T(8,128)(2,1)}), bf16[64,6,512]{2,1,0:T(8,128)(2,1)}, u32[]{:S(2)}, u32[]{:S(2)}) async-start(bf16[64,6,512]{2,1,0:T(8,128)(2,1)} %reshape.58), calls=%async_computation.4 | async-start | bytes 1048576 | tf_op jit(solution)/shard_map/all_to_all | solution.py:11
  79.0 0.0 all-reduce.3.cloned.1.call-start
  79.0 0.1 reshape.55
  79.2 1.5 fusion.9
  80.7 1.5 fusion.13
  82.2 27.7 %all-to-all-done.4 = bf16[64,6,512]{2,1,0:T(8,128)(2,1)} async-done(((bf16[64,6,512]{2,1,0:T(8,128)(2,1)}), bf16[64,6,512]{2,1,0:T(8,128)(2,1)}, u32[]{:S(2)}, u32[]{:S(2)}) %all-to-all-start.4) | async-done | bytes 393248 | tf_op jit(solution)/shard_map/all_to_all | solution.py:11
  109.9 1.2 reshape.59
  111.1 1.5 fusion.5
  112.6 0.0 all-reduce.3.cloned.1.call-update
  112.6 74.8 %all-reduce.3.cloned.1.call-done = (f32[384,768]{1,0:T(8,128)}, f32[384,768]{1,0:T(8,128)}, f32[384,768]{1,0:T(8,128)}) async-done(((f32[384,768]{1,0:T(8,128)}, f32[384,768]{1,0:T(8,128)}, f32[384,768]{1,0:T(8,128)}), (f32[384,768]{1,0:T(8,128)}, f32[384,768]{1,0:T(8,128)}, f32[384,768]{1,0:T(8,128)})) %all-reduce.3.cloned.1.call-update) | async-done | bytes 3538960 | tf_op jit(solution)/shard_map/psum | solution.py:72
  187.4 2.6 multiply_convert_fusion
  190.0 0.0 copy-start.4
  190.0 0.8 copy-done.4
  190.8 1.2 convolution_convert_fusion.4
  192.1 1.9 reshape.56
  194.0 15.9 %all-to-all-start.2 = ((bf16[64,6,512]{2,1,0:T(8,128)(2,1)}), bf16[64,6,512]{2,1,0:T(8,128)(2,1)}, u32[]{:S(2)}, u32[]{:S(2)}) async-start(bf16[64,6,512]{2,1,0:T(8,128)(2,1)} %reshape.56), calls=%async_computation.2 | async-start | bytes 1048576 | tf_op jit(solution)/shard_map/all_to_all | solution.py:18
  209.9 0.5 fusion.11
  210.4 0.6 copy-done.3
  211.0 1.2 fusion.3
  212.3 2.0 reshape.60
  214.3 28.6 %all-to-all-done.2 = bf16[64,6,512]{2,1,0:T(8,128)(2,1)} async-done(((bf16[64,6,512]{2,1,0:T(8,128)(2,1)}), bf16[64,6,512]{2,1,0:T(8,128)(2,1)}, u32[]{:S(2)}, u32[]{:S(2)}) %all-to-all-start.2) | async-done | bytes 393248 | tf_op jit(solution)/shard_map/all_to_all | solution.py:18
  242.9 6.5 %all-to-all-start.5 = ((bf16[64,6,512]{2,1,0:T(8,128)(2,1)}), bf16[64,6,512]{2,1,0:T(8,128)(2,1)}, u32[]{:S(2)}, u32[]{:S(2)}) async-start(bf16[64,6,512]{2,1,0:T(8,128)(2,1)} %reshape.60), calls=%async_computation.5 | async-start | bytes 1048576 | tf_op jit(solution)/shard_map/all_to_all | solution.py:18
  249.4 1.5 fusion.2
  250.9 1.5 fusion.1
  252.4 1.5 fusion
  253.8 1.2 reshape.57
  255.0 0.8 convolution_convert_fusion.7
  255.8 26.9 %all-to-all-done.5 = bf16[64,6,512]{2,1,0:T(8,128)(2,1)} async-done(((bf16[64,6,512]{2,1,0:T(8,128)(2,1)}), bf16[64,6,512]{2,1,0:T(8,128)(2,1)}, u32[]{:S(2)}, u32[]{:S(2)}) %all-to-all-start.5) | async-done | bytes 393248 | tf_op jit(solution)/shard_map/all_to_all | solution.py:18
  282.7 1.2 reshape.61
  283.9 0.8 convolution_convert_fusion.6
  (18 shorter events, 0.1 us)
Async XLA Ops:
  7.2 103.9 %copy-start = (bf16[1,512,768]{2,1,0:T(8,128)(2,1)S(1)}, bf16[1,512,768]{2,1,0:T(8,128)(2,1)}, u32[]{:S(2)}) copy-start(bf16[1,512,768]{2,1,0:T(8,128)(2,1)} %param.12) | copy-start | bytes 2359300
  7.2 10.1 %all-to-all-start = ((bf16[4,32,128]{2,1,0:T(8,128)(2,1)}), bf16[4,32,128]{2,1,0:T(8,128)(2,1)S(1)}, u32[]{:S(2)}, u32[]{:S(2)}) async-start(bf16[4,32,128]{2,1,0:T(8,128)(2,1)} %bitcast.57), calls=%async_computation | async-start | bytes 65536 | tf_op jit(solution)/shard_map/all_to_all | solution.py:41
  14.1 11.9 %copy-start.6 = (bf16[384,32]{0,1:T(8,128)(2,1)}, bf16[384,32]{0,1:T(8,128)(2,1)S(1)}, u32[]{:S(2)}) copy-start(bf16[384,32]{0,1:T(8,128)(2,1)S(1)} %get-tuple-element.6) | copy-start | bytes 73732
  14.1 28.6 %copy-start.8 = (bf16[384,32]{0,1:T(8,128)(2,1)}, bf16[384,32]{0,1:T(8,128)(2,1)S(1)}, u32[]{:S(2)}) copy-start(bf16[384,32]{0,1:T(8,128)(2,1)S(1)} %get-tuple-element.5) | copy-start | bytes 73732
  17.2 8.7 %all-to-all-start.3 = ((bf16[4,32,128]{2,1,0:T(8,128)(2,1)}), bf16[4,32,128]{2,1,0:T(8,128)(2,1)S(1)}, u32[]{:S(2)}, u32[]{:S(2)}) async-start(bf16[4,32,128]{2,1,0:T(8,128)(2,1)} %bitcast.58), calls=%async_computation.3 | async-start | bytes 65536 | tf_op jit(solution)/shard_map/all_to_all | solution.py:42
  25.9 47.0 %all-to-all-start.1 = ((bf16[64,6,512]{2,1,0:T(8,128)(2,1)}), bf16[64,6,512]{2,1,0:T(8,128)(2,1)S(1)}, u32[]{:S(2)}, u32[]{:S(2)}) async-start(bf16[64,6,512]{2,1,0:T(8,128)(2,1)} %reshape.54), calls=%async_computation.1 | async-start | bytes 1048576 | tf_op jit(solution)/shard_map/all_to_all | solution.py:10
  43.9 35.3 %copy-start.2 = (bf16[1,512,768]{2,1,0:T(8,128)(2,1)S(1)}, bf16[1,512,768]{2,1,0:T(8,128)(2,1)}, u32[]{:S(2)}) copy-start(bf16[1,512,768]{2,1,0:T(8,128)(2,1)} %param.11) | copy-start | bytes 2359300
  72.9 37.0 %all-to-all-start.4 = ((bf16[64,6,512]{2,1,0:T(8,128)(2,1)}), bf16[64,6,512]{2,1,0:T(8,128)(2,1)}, u32[]{:S(2)}, u32[]{:S(2)}) async-start(bf16[64,6,512]{2,1,0:T(8,128)(2,1)} %reshape.58), calls=%async_computation.4 | async-start | bytes 1048576 | tf_op jit(solution)/shard_map/all_to_all | solution.py:11
  79.0 108.4 %all-reduce.3.cloned.1.call-start = ((), (), s32[]{:S(2)}) async-start(), calls=%async_computation.6 | async-start | bytes 7077888 | tf_op jit(solution)/shard_map/psum | solution.py:72
  79.2 1.5 copy-start.1
  190.0 0.8 copy-start.4
  194.0 48.9 %all-to-all-start.2 = ((bf16[64,6,512]{2,1,0:T(8,128)(2,1)}), bf16[64,6,512]{2,1,0:T(8,128)(2,1)}, u32[]{:S(2)}, u32[]{:S(2)}) async-start(bf16[64,6,512]{2,1,0:T(8,128)(2,1)} %reshape.56), calls=%async_computation.2 | async-start | bytes 1048576 | tf_op jit(solution)/shard_map/all_to_all | solution.py:18
  209.9 1.1 copy-start.3
  212.3 37.1 %copy-start.5 = (bf16[384,768]{1,0:T(8,128)(2,1)S(1)}, bf16[384,768]{1,0:T(8,128)(2,1)}, u32[]{:S(2)}) copy-start(bf16[384,768]{1,0:T(8,128)(2,1)} %copy-done.4) | copy-start | bytes 1769476
  242.9 39.9 %all-to-all-start.5 = ((bf16[64,6,512]{2,1,0:T(8,128)(2,1)}), bf16[64,6,512]{2,1,0:T(8,128)(2,1)}, u32[]{:S(2)}, u32[]{:S(2)}) async-start(bf16[64,6,512]{2,1,0:T(8,128)(2,1)} %reshape.60), calls=%async_computation.5 | async-start | bytes 1048576 | tf_op jit(solution)/shard_map/all_to_all | solution.py:18
  252.4 2.7 copy-start.9
  253.8 30.1 %copy-start.7 = (bf16[384,32]{0,1:T(8,128)(2,1)S(1)}, bf16[384,32]{0,1:T(8,128)(2,1)}, u32[]{:S(2)}) copy-start(bf16[384,32]{0,1:T(8,128)(2,1)} %copy-done.6) | copy-start | bytes 73732
Sparse Core Ops, SparseCore 0:
  112.7 74.5 all-reduce.2
where the time goes:
time: 292 us
  waiting for transfers between devices  194 us (66%)
  starting transfers between devices  53.1 us (18%)
  matrix products  14.3 us (5%)
  between operations  14.2 us (5%)
  local copies, waits for them, and re-layouts  11.9 us (4%)
  other arithmetic  3.66 us (1%)
    psum x1, waiting for transfers between devices, shards(): pre_gate, pre_up = lax.psum((part_gate, part_up), 'dp')  74.8 us
    all_to_all x2, waiting for transfers between devices, send_back(): lax.all_to_all(shaped, ('ctx', 'tp'), split_axis=0, concat_axis=0, tiled=...  55.5 us
    all_to_all x1, waiting for transfers between devices, send_out(): lax.all_to_all(shaped[0], ('ctx', 'tp'), split_axis=0, concat_axis=0, til...  29 us
    all_to_all x1, waiting for transfers between devices, send_out(): lax.all_to_all(shaped[1], ('ctx', 'tp'), split_axis=0, concat_axis=0, til...  27.7 us
    all_to_all x2, starting transfers between devices, send_back(): lax.all_to_all(shaped, ('ctx', 'tp'), split_axis=0, concat_axis=0, tiled=...  22.4 us
    all_to_all x1, starting transfers between devices, send_out(): lax.all_to_all(shaped[0], ('ctx', 'tp'), split_axis=0, concat_axis=0, til...  16.7 us
    all_to_all x1, starting transfers between devices, send_out(): lax.all_to_all(shaped[1], ('ctx', 'tp'), split_axis=0, concat_axis=0, til...  6.1 us
    dot_general x5, matrix products, contract_first(): lax.dot_general(left, right, (((0,), (0,)), ((), ())), preferred_element_...  6.03 us
  transfers between devices with their start and end apart: 7, of which 7 were waited for; matrix products, arithmetic and copies ran while one was open for 6% of the time, Pallas kernels for 0%

commit v1 on v0

v1 whole, which is shorter than its diff:
```python
import functools

import jax
import jax.numpy as jnp
from jax import lax
from jax.experimental import pallas as pl
from jax.experimental.pallas import tpu as pltpu
from jax.sharding import PartitionSpec as P

MESH = pl.DeviceIdType.MESH
F32 = jnp.float32
BF16 = jnp.bfloat16

NZ = 16
NY = 4
NX = 4
CAP = 6
BLOCK = 128
FOLD = 32
FEAT = 128
WIDE = 512
HID = 768
HALF = 384
ROWS = 192
PIECE = 48
OWN = 4
RING = (0, 1)


def mod(a, n):
    return lax.rem(a + 2 * n, n)


def nt(a, b):
    return lax.dot_general(a, b, (((1,), (1,)), ((), ())), preferred_element_type=F32)


def tn(a, b):
    return lax.dot_general(a, b, (((0,), (0,)), ((), ())), preferred_element_type=F32)


def nn(a, b):
    return jnp.dot(a, b, preferred_element_type=F32)


def body(
    ids_ref, codes_ref, tok_ref, grd_ref, wg_hbm, wu_hbm, wd_hbm,
    lo_ref, tg_ref, gg_hbm, ug_hbm, dg_hbm,
    data, meta_in, meta, wts, code_s, rank_s, gate_s, pick, pickg, ysend, rows_in,
    xs, core_out, core_in, part, opp_out, opp_in, back_out, back_in, fwd_out, fwd_in,
    act, full, ret_out, ret_in, cmat, acc, rs_out, rs_in, wgrad,
    z_send, z_recv, my_send, my_recv, y_send, y_recv, c_send, c_recv,
    x_send, x_recv, g_send, g_recv, r_send, r_recv, s_send, s_recv, l_sem, w_sem, o_sem,
):
    dp = lax.axis_index("dp")
    z = lax.axis_index("ctx")
    y = lax.axis_index("tp")
    x = dp // 2
    core = dp - 2 * x
    z_nb = (mod(z + 1, NZ), mod(z - 1, NZ))
    x_right = mod(x + 1, NX)
    x_left = mod(x - 1, NX)
    x_opp = mod(x + 2, NX)
    peer = {"dp": 2 * x + 1 - core}

    barrier = pltpu.get_barrier_semaphore()
    for nb in z_nb:
        pl.semaphore_signal(barrier, inc=1, device_id={"ctx": nb}, device_id_type=MESH)
    for dy in range(1, NY):
        pl.semaphore_signal(barrier, inc=1, device_id={"tp": mod(y + dy, NY)}, device_id_type=MESH)
    for xn in (x_right, x_left):
        pl.semaphore_signal(barrier, inc=1, device_id={"dp": 2 * xn + core}, device_id_type=MESH)
    pl.semaphore_signal(barrier, inc=1, device_id=peer, device_id_type=MESH)

    own_copies = [
        pltpu.make_async_copy(tok_ref, data.at[0, OWN], l_sem.at[0]),
        pltpu.make_async_copy(grd_ref, data.at[1, OWN], l_sem.at[1]),
    ]
    w_copies = [
        pltpu.make_async_copy(w.at[0], wts.at[i], w_sem.at[i])
        for i, w in enumerate((wg_hbm, wu_hbm, wd_hbm))
    ]
    for cp in own_copies + w_copies:
        cp.start()
    small = jnp.concatenate([ids_ref[...].astype(F32), codes_ref[...].astype(F32)], axis=0)
    place = (
        lax.broadcasted_iota(jnp.int32, (FOLD, BLOCK), 1)
        == y * FOLD + lax.broadcasted_iota(jnp.int32, (FOLD, BLOCK), 0)
    )
    place = jnp.where(place, 1.0, 0.0).astype(BF16)
    meta_in[0] = nn(small.astype(BF16), place).astype(BF16)

    pl.semaphore_wait(barrier, 8)

    def zcopy(stream, way, s):
        if way == 0:
            src, dst = mod(OWN - s + 1, NZ), mod(OWN - s, NZ)
        else:
            src, dst = OWN + s - 1, OWN + s
        buf = meta if stream == 2 else data.at[stream]
        return pltpu.make_async_remote_copy(
            src_ref=buf.at[src], dst_ref=buf.at[dst],
            send_sem=z_send.at[stream, way, s - 1], recv_sem=z_recv.at[stream, way, s - 1],
            device_id={"ctx": z_nb[way]}, device_id_type=MESH,
        )

    def zfirst(stream, way):
        src = (tok_ref, grd_ref)[stream]
        dst = OWN - 1 if way == 0 else OWN + 1
        return pltpu.make_async_remote_copy(
            src_ref=src, dst_ref=data.at[stream, dst],
            send_sem=z_send.at[stream, way, 0], recv_sem=z_recv.at[stream, way, 0],
            device_id={"ctx": z_nb[way]}, device_id_type=MESH,
        )

    def my_copy(dy):
        return pltpu.make_async_remote_copy(
            src_ref=meta_in.at[0], dst_ref=meta_in.at[dy],
            send_sem=my_send.at[dy - 1], recv_sem=my_recv.at[dy - 1],
            device_id={"tp": mod(y + dy, NY)}, device_id_type=MESH,
        )

    for dy in range(1, NY):
        my_copy(dy).start()
    for stream in (0, 1):
        for way in RING:
            zfirst(stream, way).start()
    for dy in range(1, NY):
        my_copy(dy).wait_recv()
    total = meta_in[0].astype(F32)
    for dy in range(1, NY):
        total = total + meta_in[dy].astype(F32)
    meta[OWN] = total.astype(BF16)
    for way in RING:
        zcopy(2, way, 1).start()

    longs = ((2, 0), (0, 0), (1, 1))
    shorts = ((2, 1), (0, 1), (1, 0))

    def zstep(s):
        for pair in longs + shorts:
            zcopy(*pair, s - 1).wait_recv()
            zcopy(*pair, s).start()

    def z_loop(first, last):
        def one(s, carry):
            zstep(s)
            return carry
        lax.fori_loop(first, last + 1, one, 0)

    lane = lax.broadcasted_iota(jnp.int32, (32, BLOCK), 1)
    row = lax.broadcasted_iota(jnp.int32, (32, BLOCK), 0)

    def route(c):
        block = meta[8 * c:8 * c + 8].astype(F32)
        ids, gts = block[:, :8], block[:, 8:] * (1.0 / 256.0)
        ms, gs = [], []
        for dy in range(NY):
            e = (NY * z + mod(y + dy, NY)).astype(F32)
            hit = ids == e
            ms.append(jnp.sum(jnp.where(hit, 1.0, 0.0), axis=1))
            gs.append(jnp.sum(jnp.where(hit, gts, 0.0), axis=1))
        m = jnp.concatenate(ms, axis=0)
        g = jnp.concatenate(gs, axis=0)
        a = lax.broadcasted_iota(jnp.int32, (BLOCK, BLOCK), 0)
        b = lax.broadcasted_iota(jnp.int32, (BLOCK, BLOCK), 1)
        tri = jnp.where((a < b) & (a // FOLD == b // FOLD), 1.0, 0.0).astype(BF16)
        rank = nn(m.astype(BF16), tri)
        base = (lane // FOLD) * PIECE + (row % 8) * CAP
        code_s[c] = jnp.where(m > 0.5, base.astype(F32) + rank, -1.0)
        rank_s[c] = jnp.where(m > 0.5, rank + 1.0, 0.0)
        gate_s[c] = g

    def pickers(c):
        slot = lax.broadcasted_iota(jnp.int32, (ROWS, BLOCK), 0).astype(F32)

        def one(i, carry):
            hit = slot == code_s[c, pl.ds(i, 1), :]
            at = (
                c,
                pl.ds(pl.multiple_of((i // 8) * ROWS, ROWS), ROWS),
                pl.ds(pl.multiple_of((i % 8) * BLOCK, BLOCK), BLOCK),
            )
            pick[at] = jnp.where(hit, 1.0, 0.0).astype(BF16)
            pickg[at] = jnp.where(hit, gate_s[c, pl.ds(i, 1), :], 0.0).astype(BF16)
            return carry
        lax.fori_loop(0, 32, one, 0)

    def ycopy(c, dy):
        return pltpu.make_async_remote_copy(
            src_ref=ysend.at[c, dy], dst_ref=rows_in.at[c, y],
            send_sem=y_send.at[c, dy - 1], recv_sem=y_recv.at[c, dy - 1],
            device_id={"tp": mod(y + dy, NY)}, device_id_type=MESH,
        )

    def select(c):
        tok = data[0, 8 * c:8 * c + 8].reshape(8 * BLOCK, FEAT)
        grd = data[1, 8 * c:8 * c + 8].reshape(8 * BLOCK, FEAT)
        for dy in (2, 1, 3, 0):
            r0 = nn(pick[c, dy * ROWS:(dy + 1) * ROWS, :], tok).astype(BF16)
            r1 = nn(pickg[c, dy * ROWS:(dy + 1) * ROWS, :], grd).astype(BF16)
            if dy == 0:
                rows_in[c, y, 0] = r0
                rows_in[c, y, 1] = r1
            else:
                ysend[c, dy, 0] = r0
                ysend[c, dy, 1] = r1
                ycopy(c, dy).start()

    def combiner(c):
        et = (
            lax.broadcasted_iota(jnp.int32, (FOLD, BLOCK), 1)
            == y * FOLD + lax.broadcasted_iota(jnp.int32, (FOLD, BLOCK), 0)
        )
        et = jnp.where(et, 1.0, 0.0).astype(BF16)
        rk = nt(et, rank_s[c].astype(BF16))
        gk = nt(et, gate_s[c].astype(BF16))
        col = lax.broadcasted_iota(jnp.int32, (FOLD, 32), 1)
        base = ((col // 8) * PIECE + (col % 8) * CAP - 1).astype(F32)
        tgt = jnp.where(rk > 0.5, base + rk, -1.0)
        out_lane = lax.broadcasted_iota(jnp.int32, (FOLD, ROWS), 1).astype(F32)
        for pp in range(8):
            ones = jnp.zeros((FOLD, ROWS), F32)
            gated = jnp.zeros((FOLD, ROWS), F32)
            for q in range(NY):
                k = q * 8 + pp
                hit = out_lane == tgt[:, k:k + 1]
                ones = jnp.where(hit, 1.0, ones)
                gated = jnp.where(hit, gk[:, k:k + 1], gated)
            cmat[c, 0, pp * FOLD:(pp + 1) * FOLD, :] = gated.astype(BF16)
            cmat[c, 1, pp * FOLD:(pp + 1) * FOLD, :] = ones.astype(BF16)

    mine = pl.ds(pl.multiple_of(core * HALF, HALF), HALF)
    other = pl.ds(pl.multiple_of((1 - core) * HALF, HALF), HALF)

    def core_copy(c):
        return pltpu.make_async_remote_copy(
            src_ref=core_out.at[c], dst_ref=core_in.at[c],
            send_sem=c_send.at[c], recv_sem=c_recv.at[c],
            device_id=peer, device_id_type=MESH,
        )

    def partials(c):
        for dy in range(1, NY):
            ycopy(c, dy).wait_recv()
        for a in (0, 1):
            xs[a, c * ROWS:(c + 1) * ROWS, :] = jnp.concatenate(
                [rows_in[c, yy, a] for yy in range(NY)], axis=1
            )
        for k in range(3):
            lhs = xs[k // 2, c * ROWS:(c + 1) * ROWS, :]
            core_out[c, :, k * HALF:(k + 1) * HALF] = nn(lhs, wts[k, :, other]).astype(BF16)
        core_copy(c).start()
        for k in range(3):
            lhs = xs[k // 2, c * ROWS:(c + 1) * ROWS, :]
            part[c, :, k * HALF:(k + 1) * HALF] = nn(lhs, wts[k, :, mine])

    def x_ends(c):
        return (x_right, x_left) if c == 0 else (x_left, x_right)

    def xcopy(c, kind):
        ahead, behind = x_ends(c)
        src, dst = ((opp_out, opp_in), (back_out, back_in), (fwd_out, fwd_in))[kind]
        to = behind if kind == 1 else ahead
        return pltpu.make_async_remote_copy(
            src_ref=src.at[c], dst_ref=dst.at[c],
            send_sem=x_send.at[c, kind], recv_sem=x_recv.at[c, kind],
            device_id={"dp": 2 * to + core}, device_id_type=MESH,
        )

    def piece(c, xx):
        at = pl.ds(pl.multiple_of(xx * PIECE, PIECE), PIECE)
        return part[c, at, :] + core_in[c, at, :].astype(F32)

    def x_first(c):
        core_copy(c).wait_recv()
        ahead, behind = x_ends(c)
        opp_out[c] = piece(c, x_opp).astype(BF16)
        xcopy(c, 0).start()
        back_out[c] = piece(c, behind).astype(BF16)
        xcopy(c, 1).start()

    def x_second(c):
        ahead, behind = x_ends(c)
        xcopy(c, 0).wait_recv()
        fwd_out[c] = (piece(c, ahead) + opp_in[c].astype(F32)).astype(BF16)
        xcopy(c, 2).start()

    def gcopy(c, k):
        ahead, behind = x_ends(c)
        slot = (x, x, x, behind, behind, ahead, x_opp)[k]
        to = (
            {"dp": 2 * ahead + core}, {"dp": 2 * behind + core}, peer,
            {"dp": 2 * ahead + core}, peer, peer, peer,
        )[k]
        return pltpu.make_async_remote_copy(
            src_ref=act.at[c, core, slot], dst_ref=act.at[c, core, slot],
            send_sem=g_send.at[c, k], recv_sem=g_recv.at[c, k],
            device_id=to, device_id_type=MESH,
        )

    def x_third(c):
        xcopy(c, 1).wait_recv()
        own = piece(c, x) + back_in[c].astype(F32)
        xcopy(c, 2).wait_recv()
        own = own + fwd_in[c].astype(F32)
        pre_gate, pre_up, hid_grad = own[:, :HALF], own[:, HALF:2 * HALF], own[:, 2 * HALF:]
        squash = jax.nn.sigmoid(pre_gate)
        act[c, core, x, :, :HALF] = (pre_gate * squash * pre_up).astype(BF16)
        act[c, core, x, :, HALF:2 * HALF] = (
            hid_grad * pre_up * squash * (1.0 + pre_gate * (1.0 - squash))
        ).astype(BF16)
        act[c, core, x, :, 2 * HALF:] = (hid_grad * pre_gate * squash).astype(BF16)
        for k in (0, 1, 2):
            gcopy(c, k).start()

    def gather(c):
        gcopy(c, 0).wait_recv()
        gcopy(c, 3).start()
        gcopy(c, 4).start()
        gcopy(c, 1).wait_recv()
        gcopy(c, 5).start()

    def gather_end(c):
        gcopy(c, 3).wait_recv()
        gcopy(c, 6).start()
        for k in (2, 4, 5, 6):
            gcopy(c, k).wait_recv()

    def rcopy(c, dy):
        return pltpu.make_async_remote_copy(
            src_ref=ret_out.at[c, mod(y + dy, NY)], dst_ref=ret_in.at[c, NY - dy],
            send_sem=r_send.at[c, dy - 1], recv_sem=r_recv.at[c, dy - 1],
            device_id={"tp": mod(y + dy, NY)}, device_id_type=MESH,
        )

    def results(c):
        at = slice(c * ROWS, (c + 1) * ROWS)
        for k in range(3):
            for h in (0, 1):
                full[k, at, h * HALF:(h + 1) * HALF] = act[
                    c, h, :, :, k * HALF:(k + 1) * HALF
                ].reshape(ROWS, HALF)
        eo = nt(full[0, at, :], wts[2]).astype(BF16)
        ret_out[c, :, 0] = eo.reshape(NY, PIECE, WIDE)
        rg = (nt(full[1, at, :], wts[0]) + nt(full[2, at, :], wts[1])).astype(BF16)
        ret_out[c, :, 1] = rg.reshape(NY, PIECE, WIDE)
        for dy in (2, 1, 3):
            rcopy(c, dy).start()
        ret_in[c, 0] = ret_out[c, y]

    def combine(c):
        for dy in range(1, NY):
            rcopy(c, dy).wait_recv()
        for a in (0, 1):
            got = ret_in[c, :, a].reshape(ROWS, WIDE)
            acc[a, 256 * c:256 * c + 256, :] = nn(cmat[c, a], got)

    def weight_grad(k):
        lhs = xs[k // 2]
        rhs = full[(1, 2, 0)[k]]
        wgrad[k] = tn(lhs, rhs).astype(BF16)
        pltpu.make_async_copy(wgrad.at[k], (gg_hbm, ug_hbm, dg_hbm)[k].at[0], o_sem.at[k]).start()

    def scopy(a, way, t):
        return pltpu.make_async_remote_copy(
            src_ref=rs_out.at[a, way, t], dst_ref=rs_in.at[a, way, t],
            send_sem=s_send.at[a, way, t], recv_sem=s_recv.at[a, way, t],
            device_id={"ctx": z_nb[way]}, device_id_type=MESH,
        )

    def steps_of(a, way):
        return 8 if a == way else 7

    def term(a, way, t):
        k = steps_of(a, way) - t
        p = mod(OWN + k, NZ) if way == 0 else mod(OWN - k, NZ)
        return acc[a, pl.ds(pl.multiple_of(p * FOLD, FOLD), FOLD), :]

    def sstep(a, way, t):
        scopy(a, way, t - 1).wait_recv()
        rs_out[a, way, t] = (term(a, way, t) + rs_in[a, way, t - 1].astype(F32)).astype(BF16)
        scopy(a, way, t).start()

    z_loop(2, 5)
    for cp in own_copies:
        cp.wait()
    route(0)
    pickers(0)
    select(0)
    zstep(6)
    for cp in w_copies:
        cp.wait()
    partials(0)
    zstep(7)
    x_first(0)
    for pair in longs:
        zcopy(*pair, 7).wait_recv()
        zcopy(*pair, 8).start()
    x_second(0)
    combiner(0)
    for pair in shorts:
        zcopy(*pair, 7).wait_recv()
    zcopy(2, 0, 8).wait_recv()
    route(1)
    pickers(1)
    for pair in longs[1:]:
        zcopy(*pair, 8).wait_recv()
    select(1)
    x_third(0)
    combiner(1)
    partials(1)
    gather(0)
    x_first(1)
    gather_end(0)
    x_second(1)
    results(0)
    x_third(1)
    gather(1)
    combine(0)
    gather_end(1)
    results(1)
    weight_grad(0)
    weight_grad(1)
    weight_grad(2)
    combine(1)
    for a in (0, 1):
        for way in RING:
            rs_out[a, way, 0] = term(a, way, 0).astype(BF16)
            scopy(a, way, 0).start()

    def ring(t, carry):
        for a in (0, 1):
            for way in RING:
                sstep(a, way, t)
        return carry

    lax.fori_loop(1, 7, ring, 0)
    sstep(0, 0, 7)
    sstep(1, 1, 7)
    for a, ref in ((0, lo_ref), (1, tg_ref)):
        short = 1 - a
        scopy(a, short, 6).wait_recv()
        got = acc[a, OWN * FOLD:(OWN + 1) * FOLD, :] + rs_in[a, short, 6].astype(F32)
        scopy(a, a, 7).wait_recv()
        ref[...] = (got + rs_in[a, a, 7].astype(F32)).astype(BF16)

    for dy in range(1, NY):
        my_copy(dy).wait_send()
        for c in (0, 1):
            ycopy(c, dy).wait_send()
            rcopy(c, dy).wait_send()
    for pair in longs + shorts:
        def left(s, carry, pair=pair):
            zcopy(*pair, s).wait_send()
            return carry
        lax.fori_loop(2 if pair[0] < 2 else 1, 9 if pair in longs else 8, left, 0)
        if pair[0] < 2:
            zfirst(*pair).wait_send()
    for c in (0, 1):
        core_copy(c).wait_send()
        for kind in range(3):
            xcopy(c, kind).wait_send()
        for k in range(7):
            gcopy(c, k).wait_send()
    for a in (0, 1):
        for way in RING:
            def gone(t, carry, a=a, way=way):
                scopy(a, way, t).wait_send()
                return carry
            lax.fori_loop(0, steps_of(a, way), gone, 0)
    for k in range(3):
        pltpu.make_async_copy(
            wgrad.at[k], (gg_hbm, ug_hbm, dg_hbm)[k].at[0], o_sem.at[k]
        ).wait()


def shards(tokens, expert_ids, gate_codes, gate_weight, up_weight, down_weight, out_grad):
    vmem = pl.BlockSpec(memory_space=pltpu.VMEM)
    hbm = pl.BlockSpec(memory_space=pltpu.HBM)
    dma = pltpu.SemaphoreType.DMA
    wide3 = 3 * HALF
    scratch = [
        pltpu.VMEM((2, NZ, BLOCK, FEAT), BF16),
        pltpu.VMEM((NY, 16, BLOCK), BF16),
        pltpu.VMEM((NZ, 16, BLOCK), BF16),
        pltpu.VMEM((3, WIDE, HID), BF16),
        pltpu.VMEM((2, 32, BLOCK), F32),
        pltpu.VMEM((2, 32, BLOCK), F32),
        pltpu.VMEM((2, 32, BLOCK), F32),
        pltpu.VMEM((2, NY * ROWS, 8 * BLOCK), BF16),
        pltpu.VMEM((2, NY * ROWS, 8 * BLOCK), BF16),
        pltpu.VMEM((2, NY, 2, ROWS, FEAT), BF16),
        pltpu.VMEM((2, NY, 2, ROWS, FEAT), BF16),
        pltpu.VMEM((2, 2 * ROWS, WIDE), BF16),
        pltpu.VMEM((2, ROWS, wide3), BF16),
        pltpu.VMEM((2, ROWS, wide3), BF16),
        pltpu.VMEM((2, ROWS, wide3), F32),
    ] + [pltpu.VMEM((2, PIECE, wide3), BF16)] * 6 + [
        pltpu.VMEM((2, 2, NX, PIECE, wide3), BF16),
        pltpu.VMEM((3, 2 * ROWS, HID), BF16),
        pltpu.VMEM((2, NY, 2, PIECE, WIDE), BF16),
        pltpu.VMEM((2, NY, 2, PIECE, WIDE), BF16),
        pltpu.VMEM((2, 2, 8 * FOLD, ROWS), BF16),
        pltpu.VMEM((2, NZ * FOLD, WIDE), F32),
        pltpu.VMEM((2, 2, 8, FOLD, WIDE), BF16),
        pltpu.VMEM((2, 2, 8, FOLD, WIDE), BF16),
        pltpu.VMEM((3, WIDE, HID), BF16),
        dma((3, 2, 8)), dma((3, 2, 8)),
        dma((3,)), dma((3,)),
        dma((2, 3)), dma((2, 3)),
        dma((2,)), dma((2,)),
        dma((2, 3)), dma((2, 3)),
        dma((2, 7)), dma((2, 7)),
        dma((2, 3)), dma((2, 3)),
        dma((2, 2, 8)), dma((2, 2, 8)),
        dma((2,)), dma((3,)), dma((3,)),
    ]
    fold = jax.ShapeDtypeStruct((FOLD, WIDE), BF16)
    weight = jax.ShapeDtypeStruct((1, WIDE, HID), BF16)
    return pl.pallas_call(
        body,
        out_shape=(fold, fold, weight, weight, weight),
        in_specs=[vmem, vmem, hbm, hbm, hbm, hbm, hbm],
        out_specs=(vmem, vmem, hbm, hbm, hbm),
        scratch_shapes=scratch,
        compiler_params=pltpu.CompilerParams(
            collective_id=0, has_side_effects=True, vmem_limit_bytes=56 * 1024 * 1024
        ),
    )(
        expert_ids.T, gate_codes.T, tokens, out_grad, gate_weight, up_weight, down_weight
    )


def solution(mesh):
    placed = (
        P("ctx", ("dp", "tp")),
        P(("ctx", "tp"), None),
        P(("ctx", "tp"), None),
        P(("ctx", "tp"), "dp", None),
        P(("ctx", "tp"), "dp", None),
        P(("ctx", "tp"), "dp", None),
        P("ctx", ("dp", "tp")),
    )
    return jax.shard_map(
        shards,
        mesh=mesh,
        in_specs=placed,
        out_specs=(
            P(("ctx", "tp"), "dp"),
            P(("ctx", "tp"), "dp"),
            P(("ctx", "tp"), "dp", None),
            P(("ctx", "tp"), "dp", None),
            P(("ctx", "tp"), "dp", None),
        ),
        check_vma=False,
    )
```

time: 292 us -> 118 us (0.40)
  waiting for transfers between devices: 194 us -> 0 us
  Pallas kernels: 0 us -> 109 us
  starting transfers between devices: 53.1 us -> 0 us
  matrix products: 14.3 us -> 0 us
  between operations: 14.2 us -> 0.65 us
  local copies, waits for them, and re-layouts: 11.9 us -> 6.43 us
  other arithmetic: 3.66 us -> 0 us
    all_to_all x6 -> x0, waiting for transfers between devices: 120 us -> none  [the longest x2 55.5 us: send_back(): lax.all_to_all(shaped, ('ctx', 'tp'), split_axis=0, concat_axis=0, tiled=...]
    pallas_call x0 -> x1, Pallas kernels: none -> 109 us  [shards(): pl.pallas_call(body, out_shape=(fold, fold, weight, weight, weight), in_s...]
    psum x1 -> x0, waiting for transfers between devices: 74.8 us -> none  [shards(): pre_gate, pre_up = lax.psum((part_gate, part_up), 'dp')]
    all_to_all x6 -> x0, starting transfers between devices: 53.1 us -> none  [the longest x2 22.4 us: send_back(): lax.all_to_all(shaped, ('ctx', 'tp'), split_axis=0, concat_axis=0, tiled=...]
    dot_general x14 -> x0, matrix products: 14.3 us -> none  [the longest x5 6.03 us: contract_first(): lax.dot_general(left, right, (((0,), (0,)), ((), ())), preferred_element_...]
    reshape x8 -> x0, local copies, waits for them, and re-layouts: 9.44 us -> none  [the longest x2 3.93 us: send_back(): shaped = payload.reshape(n_ctx * n_tp, -1, payload.shape[-1])]
    unnamed x21 -> x11, local copies, waits for them, and re-layouts: 2.23 us -> 6.43 us
  transfers between devices with their start and end apart: 7 -> 0, of which waited for: 7 -> 0; matrix products, arithmetic and copies ran while one was open for 6% -> 0% of each run, Pallas kernels for 0% -> 0%
where the time goes in v1:
time: 118 us; the launch traced here: 116 us
  Pallas kernels  109 us (92%)
  local copies, waits for them, and re-layouts  6.43 us (5%)
    pallas_call x1, Pallas kernels, shards(): pl.pallas_call(body, out_shape=(fold, fold, weight, weight, weight), in_s...  109 us
    unnamed x11, local copies, waits for them, and re-layouts  6.43 us

profile of v1, /device:TPU:6, one launch (start us, length us, event | category | flops | bytes accessed | tf_op | source)
XLA Modules:
  0.0 115.8 jit_solution(15105403026063181390)
XLA Ops:
  0.6 108.7 %shard_map.110 = (bf16[32,512]{1,0:T(8,128)(2,1)}, bf16[32,512]{1,0:T(8,128)(2,1)}, bf16[1,512,768]{2,1,0:T(8,128)(2,1)}, bf16[1,512,768]{2,1,0:T(8,128)(2,1)}, bf16[1,512,768]{2,1,0:T(8,128)(2,1)}) custom-call(s32[8,32]{1,0:T(8,128)} %bitcast.2, s32[8,32]{1,0:T(8,128)} %bitcast.3, bf16[128,128]{1,0:T(8,128)(2,1)} %tok_ref.1, bf16[128,128]{1,0:T(8,128)(2,1)} %grd_ref.1, ...), custom_call_target="tpu_custom_call" | custom-call | tf_op jit(solution)/shard_map/pallas_call | solution.py:521
  109.3 0.0 copy-start.2
  109.3 1.4 %copy.17 = bf16[32,512]{1,0:T(8,128)(2,1)} copy(bf16[32,512]{1,0:T(8,128)(2,1)} %get-tuple-element.10) | data formatting | bytes 65536
  110.7 0.0 copy-done.2
  110.7 0.6 copy.18
  111.3 0.0 copy-start.1
  111.3 2.1 %copy.19 = bf16[1,512,768]{2,1,0:T(8,128)(2,1)} copy(bf16[1,512,768]{2,1,0:T(8,128)(2,1)} %get-tuple-element.12) | data formatting | bytes 1572864
  113.5 0.0 copy-done.1
  113.5 0.0 copy-start
  113.5 0.9 copy.20
  114.4 0.5 copy-done
  114.9 0.9 copy.21
Async XLA Ops:
  109.3 1.4 %copy-start.2 = (bf16[32,512]{1,0:T(8,128)(2,1)S(1)}, bf16[32,512]{1,0:T(8,128)(2,1)}, u32[]{:S(2)}) copy-start(bf16[32,512]{1,0:T(8,128)(2,1)} %get-tuple-element.11) | copy-start | bytes 98308
  111.3 2.1 %copy-start.1 = (bf16[1,512,768]{2,1,0:T(8,128)(2,1)S(1)}, bf16[1,512,768]{2,1,0:T(8,128)(2,1)}, u32[]{:S(2)}) copy-start(bf16[1,512,768]{2,1,0:T(8,128)(2,1)} %get-tuple-element.13) | copy-start | bytes 2359300
  113.5 1.4 %copy-start = (bf16[1,512,768]{2,1,0:T(8,128)(2,1)S(1)}, bf16[1,512,768]{2,1,0:T(8,128)(2,1)}, u32[]{:S(2)}) copy-start(bf16[1,512,768]{2,1,0:T(8,128)(2,1)} %get-tuple-element.14) | copy-start | bytes 2359300

commit v2 on v1

--- a/solution.py
+++ b/solution.py
@@ -58,13 +58,14 @@
     x = dp // 2
     core = dp - 2 * x
     z_nb = (mod(z + 1, NZ), mod(z - 1, NZ))
+    z_nb2 = (mod(z + 2, NZ), mod(z - 2, NZ))
     x_right = mod(x + 1, NX)
     x_left = mod(x - 1, NX)
     x_opp = mod(x + 2, NX)
     peer = {"dp": 2 * x + 1 - core}
 
     barrier = pltpu.get_barrier_semaphore()
-    for nb in z_nb:
+    for nb in z_nb + z_nb2:
         pl.semaphore_signal(barrier, inc=1, device_id={"ctx": nb}, device_id_type=MESH)
     for dy in range(1, NY):
         pl.semaphore_signal(barrier, inc=1, device_id={"tp": mod(y + dy, NY)}, device_id_type=MESH)
@@ -90,28 +91,26 @@
     place = jnp.where(place, 1.0, 0.0).astype(BF16)
     meta_in[0] = nn(small.astype(BF16), place).astype(BF16)
 
-    pl.semaphore_wait(barrier, 8)
-
-    def zcopy(stream, way, s):
-        if way == 0:
-            src, dst = mod(OWN - s + 1, NZ), mod(OWN - s, NZ)
+    pl.semaphore_wait(barrier, 10)
+
+    def at_distance(way, d):
+        return (OWN - d) % NZ if way == 0 else (OWN + d) % NZ
+
+    def zcopy(stream, way, d):
+        hop = 2 if d % 2 == 0 else 1
+        buf = meta if stream == 2 else data.at[stream]
+        if d == hop and stream < 2:
+            src = (tok_ref, grd_ref)[stream]
         else:
-            src, dst = OWN + s - 1, OWN + s
-        buf = meta if stream == 2 else data.at[stream]
-        return pltpu.make_async_remote_copy(
-            src_ref=buf.at[src], dst_ref=buf.at[dst],
-            send_sem=z_send.at[stream, way, s - 1], recv_sem=z_recv.at[stream, way, s - 1],
-            device_id={"ctx": z_nb[way]}, device_id_type=MESH,
-        )
-
-    def zfirst(stream, way):
-        src = (tok_ref, grd_ref)[stream]
-        dst = OWN - 1 if way == 0 else OWN + 1
-        return pltpu.make_async_remote_copy(
-            src_ref=src, dst_ref=data.at[stream, dst],
-            send_sem=z_send.at[stream, way, 0], recv_sem=z_recv.at[stream, way, 0],
-            device_id={"ctx": z_nb[way]}, device_id_type=MESH,
-        )
+            src = buf.at[at_distance(way, d - hop)]
+        return pltpu.make_async_remote_copy(
+            src_ref=src, dst_ref=buf.at[at_distance(way, d)],
+            send_sem=z_send.at[stream, way, d - 1], recv_sem=z_recv.at[stream, way, d - 1],
+            device_id={"ctx": (z_nb, z_nb2)[hop - 1][way]}, device_id_type=MESH,
+        )
+
+    def reach(stream, way):
+        return 8 if (stream == 1) == (way == 1) else 7
 
     def my_copy(dy):
         return pltpu.make_async_remote_copy(
@@ -122,31 +121,35 @@
 
     for dy in range(1, NY):
         my_copy(dy).start()
-    for stream in (0, 1):
-        for way in RING:
-            zfirst(stream, way).start()
+    values = ((0, 0), (1, 1), (0, 1), (1, 0))
+    routes = ((2, 0), (2, 1))
+    for pair in values:
+        zcopy(*pair, 2).start()
+    for pair in values:
+        zcopy(*pair, 1).start()
     for dy in range(1, NY):
         my_copy(dy).wait_recv()
     total = meta_in[0].astype(F32)
     for dy in range(1, NY):
         total = total + meta_in[dy].astype(F32)
     meta[OWN] = total.astype(BF16)
-    for way in RING:
-        zcopy(2, way, 1).start()
-
-    longs = ((2, 0), (0, 0), (1, 1))
-    shorts = ((2, 1), (0, 1), (1, 0))
-
-    def zstep(s):
-        for pair in longs + shorts:
-            zcopy(*pair, s - 1).wait_recv()
-            zcopy(*pair, s).start()
-
-    def z_loop(first, last):
-        def one(s, carry):
-            zstep(s)
-            return carry
-        lax.fori_loop(first, last + 1, one, 0)
+    for pair in routes:
+        zcopy(*pair, 2).start()
+        zcopy(*pair, 1).start()
+
+    def relay(d):
+        for pair in routes + values:
+            zcopy(*pair, d).wait_recv()
+            if d + 2 <= reach(*pair):
+                zcopy(*pair, d + 2).start()
+        for pair in routes + values:
+            zcopy(*pair, d + 1).start()
+
+    def arrived(pairs, first, last):
+        for pair in pairs:
+            for d in range(first, min(last, reach(*pair)) + 1):
+                if d % 2 == 1 or d == 8:
+                    zcopy(*pair, d).wait_recv()
 
     lane = lax.broadcasted_iota(jnp.int32, (32, BLOCK), 1)
     row = lax.broadcasted_iota(jnp.int32, (32, BLOCK), 0)
@@ -233,10 +236,10 @@
     mine = pl.ds(pl.multiple_of(core * HALF, HALF), HALF)
     other = pl.ds(pl.multiple_of((1 - core) * HALF, HALF), HALF)
 
-    def core_copy(c):
-        return pltpu.make_async_remote_copy(
-            src_ref=core_out.at[c], dst_ref=core_in.at[c],
-            send_sem=c_send.at[c], recv_sem=c_recv.at[c],
+    def core_copy(c, k):
+        return pltpu.make_async_remote_copy(
+            src_ref=core_out.at[c, k], dst_ref=core_in.at[c, k],
+            send_sem=c_send.at[c, k], recv_sem=c_recv.at[c, k],
             device_id=peer, device_id_type=MESH,
         )
 
@@ -249,42 +252,44 @@
             )
         for k in range(3):
             lhs = xs[k // 2, c * ROWS:(c + 1) * ROWS, :]
-            core_out[c, :, k * HALF:(k + 1) * HALF] = nn(lhs, wts[k, :, other]).astype(BF16)
-        core_copy(c).start()
+            core_out[c, k] = nn(lhs, wts[k, :, other]).astype(BF16)
+            core_copy(c, k).start()
         for k in range(3):
             lhs = xs[k // 2, c * ROWS:(c + 1) * ROWS, :]
-            part[c, :, k * HALF:(k + 1) * HALF] = nn(lhs, wts[k, :, mine])
+            part[c, k] = nn(lhs, wts[k, :, mine])
 
     def x_ends(c):
         return (x_right, x_left) if c == 0 else (x_left, x_right)
 
-    def xcopy(c, kind):
+    def xcopy(c, kind, k):
         ahead, behind = x_ends(c)
         src, dst = ((opp_out, opp_in), (back_out, back_in), (fwd_out, fwd_in))[kind]
         to = behind if kind == 1 else ahead
         return pltpu.make_async_remote_copy(
-            src_ref=src.at[c], dst_ref=dst.at[c],
-            send_sem=x_send.at[c, kind], recv_sem=x_recv.at[c, kind],
+            src_ref=src.at[c, k], dst_ref=dst.at[c, k],
+            send_sem=x_send.at[c, kind, k], recv_sem=x_recv.at[c, kind, k],
             device_id={"dp": 2 * to + core}, device_id_type=MESH,
         )
 
-    def piece(c, xx):
+    def piece(c, k, xx):
         at = pl.ds(pl.multiple_of(xx * PIECE, PIECE), PIECE)
-        return part[c, at, :] + core_in[c, at, :].astype(F32)
+        return part[c, k, at, :] + core_in[c, k, at, :].astype(F32)
 
     def x_first(c):
-        core_copy(c).wait_recv()
         ahead, behind = x_ends(c)
-        opp_out[c] = piece(c, x_opp).astype(BF16)
-        xcopy(c, 0).start()
-        back_out[c] = piece(c, behind).astype(BF16)
-        xcopy(c, 1).start()
+        for k in range(3):
+            core_copy(c, k).wait_recv()
+            opp_out[c, k] = piece(c, k, x_opp).astype(BF16)
+            xcopy(c, 0, k).start()
+            back_out[c, k] = piece(c, k, behind).astype(BF16)
+            xcopy(c, 1, k).start()
 
     def x_second(c):
         ahead, behind = x_ends(c)
-        xcopy(c, 0).wait_recv()
-        fwd_out[c] = (piece(c, ahead) + opp_in[c].astype(F32)).astype(BF16)
-        xcopy(c, 2).start()
+        for k in range(3):
+            xcopy(c, 0, k).wait_recv()
+            fwd_out[c, k] = (piece(c, k, ahead) + opp_in[c, k].astype(F32)).astype(BF16)
+            xcopy(c, 2, k).start()
 
     def gcopy(c, k):
         ahead, behind = x_ends(c)
@@ -300,11 +305,14 @@
         )
 
     def x_third(c):
-        xcopy(c, 1).wait_recv()
-        own = piece(c, x) + back_in[c].astype(F32)
-        xcopy(c, 2).wait_recv()
-        own = own + fwd_in[c].astype(F32)
-        pre_gate, pre_up, hid_grad = own[:, :HALF], own[:, HALF:2 * HALF], own[:, 2 * HALF:]
+        sums = []
+        for k in range(3):
+            xcopy(c, 1, k).wait_recv()
+            xcopy(c, 2, k).wait_recv()
+            sums.append(
+                piece(c, k, x) + back_in[c, k].astype(F32) + fwd_in[c, k].astype(F32)
+            )
+        pre_gate, pre_up, hid_grad = sums
         squash = jax.nn.sigmoid(pre_gate)
         act[c, core, x, :, :HALF] = (pre_gate * squash * pre_up).astype(BF16)
         act[c, core, x, :, HALF:2 * HALF] = (
@@ -362,117 +370,120 @@
         wgrad[k] = tn(lhs, rhs).astype(BF16)
         pltpu.make_async_copy(wgrad.at[k], (gg_hbm, ug_hbm, dg_hbm)[k].at[0], o_sem.at[k]).start()
 
-    def scopy(a, way, t):
-        return pltpu.make_async_remote_copy(
-            src_ref=rs_out.at[a, way, t], dst_ref=rs_in.at[a, way, t],
-            send_sem=s_send.at[a, way, t], recv_sem=s_recv.at[a, way, t],
-            device_id={"ctx": z_nb[way]}, device_id_type=MESH,
-        )
-
-    def steps_of(a, way):
+    def scopy(a, way, d):
+        hop = 2 if d % 2 == 0 else 1
+        return pltpu.make_async_remote_copy(
+            src_ref=rs_out.at[a, way, d - 1], dst_ref=rs_in.at[a, way, d - 1],
+            send_sem=s_send.at[a, way, d - 1], recv_sem=s_recv.at[a, way, d - 1],
+            device_id={"ctx": (z_nb, z_nb2)[hop - 1][way]}, device_id_type=MESH,
+        )
+
+    def span(a, way):
         return 8 if a == way else 7
 
-    def term(a, way, t):
-        k = steps_of(a, way) - t
-        p = mod(OWN + k, NZ) if way == 0 else mod(OWN - k, NZ)
-        return acc[a, pl.ds(pl.multiple_of(p * FOLD, FOLD), FOLD), :]
-
-    def sstep(a, way, t):
-        scopy(a, way, t - 1).wait_recv()
-        rs_out[a, way, t] = (term(a, way, t) + rs_in[a, way, t - 1].astype(F32)).astype(BF16)
-        scopy(a, way, t).start()
-
-    z_loop(2, 5)
+    def collected(a, way, d):
+        p = (OWN + d) % NZ if way == 0 else (OWN - d) % NZ
+        value = acc[a, p * FOLD:(p + 1) * FOLD, :]
+        if d % 2 == 0:
+            for e in (d + 1, d + 2):
+                if e <= span(a, way):
+                    scopy(a, way, e).wait_recv()
+                    value = value + rs_in[a, way, e - 1].astype(F32)
+        return value
+
+    flows = ((0, 0), (1, 1), (0, 1), (1, 0))
+
+    def send_sums(d):
+        for a, way in flows:
+            if d <= span(a, way):
+                rs_out[a, way, d - 1] = collected(a, way, d).astype(BF16)
+                scopy(a, way, d).start()
+
+    relay(2)
+    relay(4)
+    arrived(routes, 1, 4)
+    route(0)
+    pickers(0)
+    relay(6)
     for cp in own_copies:
         cp.wait()
-    route(0)
-    pickers(0)
+    arrived(values, 1, 4)
     select(0)
-    zstep(6)
+    arrived(routes, 5, 8)
+    route(1)
+    pickers(1)
+    arrived(values, 5, 8)
+    select(1)
     for cp in w_copies:
         cp.wait()
     partials(0)
-    zstep(7)
+    combiner(0)
     x_first(0)
-    for pair in longs:
-        zcopy(*pair, 7).wait_recv()
-        zcopy(*pair, 8).start()
+    partials(1)
     x_second(0)
-    combiner(0)
-    for pair in shorts:
-        zcopy(*pair, 7).wait_recv()
-    zcopy(2, 0, 8).wait_recv()
-    route(1)
-    pickers(1)
-    for pair in longs[1:]:
-        zcopy(*pair, 8).wait_recv()
-    select(1)
+    x_first(1)
+    combiner(1)
     x_third(0)
-    combiner(1)
-    partials(1)
+    x_second(1)
     gather(0)
-    x_first(1)
+    x_third(1)
     gather_end(0)
-    x_second(1)
     results(0)
-    x_third(1)
     gather(1)
-    combine(0)
     gather_end(1)
     results(1)
     weight_grad(0)
+    combine(0)
     weight_grad(1)
     weight_grad(2)
     combine(1)
-    for a in (0, 1):
+    send_sums(8)
+    send_sums(7)
+    for d in (6, 5, 4, 3, 2, 1):
+        send_sums(d)
+    for a, ref in ((0, lo_ref), (1, tg_ref)):
+        value = acc[a, OWN * FOLD:(OWN + 1) * FOLD, :]
         for way in RING:
-            rs_out[a, way, 0] = term(a, way, 0).astype(BF16)
-            scopy(a, way, 0).start()
-
-    def ring(t, carry):
-        for a in (0, 1):
-            for way in RING:
-                sstep(a, way, t)
-        return carry
-
-    lax.fori_loop(1, 7, ring, 0)
-    sstep(0, 0, 7)
-    sstep(1, 1, 7)
-    for a, ref in ((0, lo_ref), (1, tg_ref)):
-        short = 1 - a
-        scopy(a, short, 6).wait_recv()
-        got = acc[a, OWN * FOLD:(OWN + 1) * FOLD, :] + rs_in[a, short, 6].astype(F32)
-        scopy(a, a, 7).wait_recv()
-        ref[...] = (got + rs_in[a, a, 7].astype(F32)).astype(BF16)
+            for d in (1, 2):
+                scopy(a, way, d).wait_recv()
+                value = value + rs_in[a, way, d - 1].astype(F32)
+        ref[...] = value.astype(BF16)
 
     for dy in range(1, NY):
         my_copy(dy).wait_send()
         for c in (0, 1):
             ycopy(c, dy).wait_send()
             rcopy(c, dy).wait_send()
-    for pair in longs + shorts:
-        def left(s, carry, pair=pair):
-            zcopy(*pair, s).wait_send()
-            return carry
-        lax.fori_loop(2 if pair[0] < 2 else 1, 9 if pair in longs else 8, left, 0)
-        if pair[0] < 2:
-            zfirst(*pair).wait_send()
+    for pair in routes + values:
+        for d in range(1, reach(*pair) + 1):
+            zcopy(*pair, d).wait_send()
     for c in (0, 1):
-        core_copy(c).wait_send()
-        for kind in range(3):
-            xcopy(c, kind).wait_send()
+        for k in range(3):
+            core_copy(c, k).wait_send()
+            for kind in range(3):
+                xcopy(c, kind, k).wait_send()
         for k in range(7):
             gcopy(c, k).wait_send()
-    for a in (0, 1):
-        for way in RING:
-            def gone(t, carry, a=a, way=way):
-                scopy(a, way, t).wait_send()
-                return carry
-            lax.fori_loop(0, steps_of(a, way), gone, 0)
+    for a, way in flows:
+        for d in range(1, span(a, way) + 1):
+            scopy(a, way, d).wait_send()
     for k in range(3):
         pltpu.make_async_copy(
             wgrad.at[k], (gg_hbm, ug_hbm, dg_hbm)[k].at[0], o_sem.at[k]
         ).wait()
+
+
+def keep_body(*refs):
+    sources, results, held, sems = refs[:5], refs[5:10], refs[10:15], refs[15]
+    into = [pltpu.make_async_copy(sources[i], held[i], sems.at[0, i]) for i in range(5)]
+    out = [pltpu.make_async_copy(held[i], results[i], sems.at[1, i]) for i in range(5)]
+    for cp in into:
+        cp.start()
+    for first, second in zip(into, out):
+        first.wait()
+        second.start()
+    for cp in out:
+        cp.wait()
 
 
 def shards(tokens, expert_ids, gate_codes, gate_weight, up_weight, down_weight, out_grad):
@@ -493,10 +504,10 @@
         pltpu.VMEM((2, NY, 2, ROWS, FEAT), BF16),
         pltpu.VMEM((2, NY, 2, ROWS, FEAT), BF16),
         pltpu.VMEM((2, 2 * ROWS, WIDE), BF16),
-        pltpu.VMEM((2, ROWS, wide3), BF16),
-        pltpu.VMEM((2, ROWS, wide3), BF16),
-        pltpu.VMEM((2, ROWS, wide3), F32),
-    ] + [pltpu.VMEM((2, PIECE, wide3), BF16)] * 6 + [
+        pltpu.VMEM((2, 3, ROWS, HALF), BF16),
+        pltpu.VMEM((2, 3, ROWS, HALF), BF16),
+        pltpu.VMEM((2, 3, ROWS, HALF), F32),
+    ] + [pltpu.VMEM((2, 3, PIECE, HALF), BF16)] * 6 + [
         pltpu.VMEM((2, 2, NX, PIECE, wide3), BF16),
         pltpu.VMEM((3, 2 * ROWS, HID), BF16),
         pltpu.VMEM((2, NY, 2, PIECE, WIDE), BF16),
@@ -509,8 +520,8 @@
         dma((3, 2, 8)), dma((3, 2, 8)),
         dma((3,)), dma((3,)),
         dma((2, 3)), dma((2, 3)),
-        dma((2,)), dma((2,)),
         dma((2, 3)), dma((2, 3)),
+        dma((2, 3, 3)), dma((2, 3, 3)),
         dma((2, 7)), dma((2, 7)),
         dma((2, 3)), dma((2, 3)),
         dma((2, 2, 8)), dma((2, 2, 8)),
@@ -518,7 +529,8 @@
     ]
     fold = jax.ShapeDtypeStruct((FOLD, WIDE), BF16)
     weight = jax.ShapeDtypeStruct((1, WIDE, HID), BF16)
-    return pl.pallas_call(
+    hbm5 = (hbm,) * 5
+    results = pl.pallas_call(
         body,
         out_shape=(fold, fold, weight, weight, weight),
         in_specs=[vmem, vmem, hbm, hbm, hbm, hbm, hbm],
@@ -530,6 +542,14 @@
     )(
         expert_ids.T, gate_codes.T, tokens, out_grad, gate_weight, up_weight, down_weight
     )
+    return pl.pallas_call(
+        keep_body,
+        out_shape=(fold, fold, weight, weight, weight),
+        in_specs=hbm5,
+        out_specs=hbm5,
+        scratch_shapes=[pltpu.VMEM(out.shape, BF16) for out in (fold, fold, weight, weight, weight)]
+        + [dma((2, 5))],
+    )(*results)
 
 
 def solution(mesh):

time: 118 us -> 100 us (0.85)
  Pallas kernels: 109 us -> 98.3 us
  local copies, waits for them, and re-layouts: 6.43 us -> 0 us
    pallas_call x1, Pallas kernels: 109 us -> 95.6 us  [shards(): pl.pallas_call(body, out_shape=(fold, fold, weight, weight, weight), in_s...]
    unnamed x11 -> x0, local copies, waits for them, and re-layouts: 6.43 us -> none
    pallas_call x0 -> x1, Pallas kernels: none -> 2.66 us  [shards(): pl.pallas_call(keep_body, out_shape=(fold, fold, weight, weight, weight),...]
where the time goes in v2:
time: 100 us; the launch traced here: 98.9 us
  Pallas kernels  98.3 us (98%)
    pallas_call x1, Pallas kernels, shards(): pl.pallas_call(body, out_shape=(fold, fold, weight, weight, weight), in_s...  95.6 us
    pallas_call x1, Pallas kernels, shards(): pl.pallas_call(keep_body, out_shape=(fold, fold, weight, weight, weight),...  2.66 us

profile of v2, /device:TPU:6, one launch (start us, length us, event | category | flops | bytes accessed | tf_op | source)
XLA Modules:
  0.0 98.9 jit_solution(4170703795490878787)
XLA Ops:
  0.6 95.6 %shard_map.110 = (bf16[32,512]{1,0:T(8,128)(2,1)}, bf16[32,512]{1,0:T(8,128)(2,1)}, bf16[1,512,768]{2,1,0:T(8,128)(2,1)}, bf16[1,512,768]{2,1,0:T(8,128)(2,1)}, bf16[1,512,768]{2,1,0:T(8,128)(2,1)}) custom-call(s32[8,32]{1,0:T(8,128)} %bitcast.2, s32[8,32]{1,0:T(8,128)} %bitcast.3, bf16[128,128]{1,0:T(8,128)(2,1)} %tok_ref.1, bf16[128,128]{1,0:T(8,128)(2,1)} %grd_ref.1, ...), custom_call_target="tpu_custom_call" | custom-call | tf_op jit(solution)/shard_map/pallas_call | solution.py:533
  96.3 2.7 %shard_map.111 = (bf16[32,512]{1,0:T(8,128)(2,1)}, bf16[32,512]{1,0:T(8,128)(2,1)}, bf16[1,512,768]{2,1,0:T(8,128)(2,1)}, bf16[1,512,768]{2,1,0:T(8,128)(2,1)}, bf16[1,512,768]{2,1,0:T(8,128)(2,1)}) custom-call(bf16[32,512]{1,0:T(8,128)(2,1)} %get-tuple-element.10.refs_0_, bf16[32,512]{1,0:T(8,128)(2,1)} %get-tuple-element.11.refs_1_, ...), custom_call_target="tpu_custom_call" | custom-call | tf_op jit(solution)/shard_map/pallas_call | solution.py:545

commit v3 on v2

--- a/solution.py
+++ b/solution.py
@@ -48,7 +48,7 @@
     lo_ref, tg_ref, gg_hbm, ug_hbm, dg_hbm,
     data, meta_in, meta, wts, code_s, rank_s, gate_s, pick, pickg, ysend, rows_in,
     xs, core_out, core_in, part, opp_out, opp_in, back_out, back_in, fwd_out, fwd_in,
-    act, full, ret_out, ret_in, cmat, acc, rs_out, rs_in, wgrad,
+    gu, act, full, ret_out, ret_in, cmat, acc, rs_out, rs_in, wgrad,
     z_send, z_recv, my_send, my_recv, y_send, y_recv, c_send, c_recv,
     x_send, x_recv, g_send, g_recv, r_send, r_recv, s_send, s_recv, l_sem, w_sem, o_sem,
 ):
@@ -121,12 +121,13 @@
 
     for dy in range(1, NY):
         my_copy(dy).start()
-    values = ((0, 0), (1, 1), (0, 1), (1, 0))
+    toks = ((0, 0), (0, 1))
+    grds = ((1, 1), (1, 0))
     routes = ((2, 0), (2, 1))
-    for pair in values:
-        zcopy(*pair, 2).start()
-    for pair in values:
-        zcopy(*pair, 1).start()
+    for pairs in (toks, grds):
+        for d in (2, 1):
+            for pair in pairs:
+                zcopy(*pair, d).start()
     for dy in range(1, NY):
         my_copy(dy).wait_recv()
     total = meta_in[0].astype(F32)
@@ -137,12 +138,12 @@
         zcopy(*pair, 2).start()
         zcopy(*pair, 1).start()
 
-    def relay(d):
-        for pair in routes + values:
+    def relay(pairs, d):
+        for pair in pairs:
             zcopy(*pair, d).wait_recv()
             if d + 2 <= reach(*pair):
                 zcopy(*pair, d + 2).start()
-        for pair in routes + values:
+        for pair in pairs:
             zcopy(*pair, d + 1).start()
 
     def arrived(pairs, first, last):
@@ -189,26 +190,23 @@
             return carry
         lax.fori_loop(0, 32, one, 0)
 
-    def ycopy(c, dy):
-        return pltpu.make_async_remote_copy(
-            src_ref=ysend.at[c, dy], dst_ref=rows_in.at[c, y],
-            send_sem=y_send.at[c, dy - 1], recv_sem=y_recv.at[c, dy - 1],
+    def ycopy(c, dy, a):
+        return pltpu.make_async_remote_copy(
+            src_ref=ysend.at[c, dy, a], dst_ref=rows_in.at[c, y, a],
+            send_sem=y_send.at[c, dy - 1, a], recv_sem=y_recv.at[c, dy - 1, a],
             device_id={"tp": mod(y + dy, NY)}, device_id_type=MESH,
         )
 
-    def select(c):
-        tok = data[0, 8 * c:8 * c + 8].reshape(8 * BLOCK, FEAT)
-        grd = data[1, 8 * c:8 * c + 8].reshape(8 * BLOCK, FEAT)
+    def select(c, a):
+        rows = data[a, 8 * c:8 * c + 8].reshape(8 * BLOCK, FEAT)
+        picks = (pick, pickg)[a]
         for dy in (2, 1, 3, 0):
-            r0 = nn(pick[c, dy * ROWS:(dy + 1) * ROWS, :], tok).astype(BF16)
-            r1 = nn(pickg[c, dy * ROWS:(dy + 1) * ROWS, :], grd).astype(BF16)
+            got = nn(picks[c, dy * ROWS:(dy + 1) * ROWS, :], rows).astype(BF16)
             if dy == 0:
-                rows_in[c, y, 0] = r0
-                rows_in[c, y, 1] = r1
+                rows_in[c, y, a] = got
             else:
-                ysend[c, dy, 0] = r0
-                ysend[c, dy, 1] = r1
-                ycopy(c, dy).start()
+                ysend[c, dy, a] = got
+                ycopy(c, dy, a).start()
 
     def combiner(c):
         et = (
@@ -243,26 +241,23 @@
             device_id=peer, device_id_type=MESH,
         )
 
-    def partials(c):
+    def partials(c, a):
+        at = slice(c * ROWS, (c + 1) * ROWS)
         for dy in range(1, NY):
-            ycopy(c, dy).wait_recv()
-        for a in (0, 1):
-            xs[a, c * ROWS:(c + 1) * ROWS, :] = jnp.concatenate(
-                [rows_in[c, yy, a] for yy in range(NY)], axis=1
-            )
-        for k in range(3):
-            lhs = xs[k // 2, c * ROWS:(c + 1) * ROWS, :]
+            ycopy(c, dy, a).wait_recv()
+        lhs = jnp.concatenate([rows_in[c, yy, a] for yy in range(NY)], axis=1)
+        xs[a, at, :] = lhs
+        for k in ((0, 1), (2,))[a]:
             core_out[c, k] = nn(lhs, wts[k, :, other]).astype(BF16)
             core_copy(c, k).start()
-        for k in range(3):
-            lhs = xs[k // 2, c * ROWS:(c + 1) * ROWS, :]
+        for k in ((0, 1), (2,))[a]:
             part[c, k] = nn(lhs, wts[k, :, mine])
 
-    def x_ends(c):
-        return (x_right, x_left) if c == 0 else (x_left, x_right)
+    def x_ends(c, k):
+        return (x_right, x_left) if (c + k) % 2 == 0 else (x_left, x_right)
 
     def xcopy(c, kind, k):
-        ahead, behind = x_ends(c)
+        ahead, behind = x_ends(c, k)
         src, dst = ((opp_out, opp_in), (back_out, back_in), (fwd_out, fwd_in))[kind]
         to = behind if kind == 1 else ahead
         return pltpu.make_async_remote_copy(
@@ -275,94 +270,98 @@
         at = pl.ds(pl.multiple_of(xx * PIECE, PIECE), PIECE)
         return part[c, k, at, :] + core_in[c, k, at, :].astype(F32)
 
-    def x_first(c):
-        ahead, behind = x_ends(c)
-        for k in range(3):
-            core_copy(c, k).wait_recv()
-            opp_out[c, k] = piece(c, k, x_opp).astype(BF16)
-            xcopy(c, 0, k).start()
-            back_out[c, k] = piece(c, k, behind).astype(BF16)
-            xcopy(c, 1, k).start()
-
-    def x_second(c):
-        ahead, behind = x_ends(c)
-        for k in range(3):
-            xcopy(c, 0, k).wait_recv()
-            fwd_out[c, k] = (piece(c, k, ahead) + opp_in[c, k].astype(F32)).astype(BF16)
-            xcopy(c, 2, k).start()
-
-    def gcopy(c, k):
-        ahead, behind = x_ends(c)
-        slot = (x, x, x, behind, behind, ahead, x_opp)[k]
+    def x_first(c, k):
+        core_copy(c, k).wait_recv()
+        opp_out[c, k] = piece(c, k, x_opp).astype(BF16)
+        xcopy(c, 0, k).start()
+        back_out[c, k] = piece(c, k, x_ends(c, k)[1]).astype(BF16)
+        xcopy(c, 1, k).start()
+
+    def x_second(c, k):
+        xcopy(c, 0, k).wait_recv()
+        ahead = x_ends(c, k)[0]
+        fwd_out[c, k] = (piece(c, k, ahead) + opp_in[c, k].astype(F32)).astype(BF16)
+        xcopy(c, 2, k).start()
+
+    def x_sum(c, k):
+        xcopy(c, 1, k).wait_recv()
+        xcopy(c, 2, k).wait_recv()
+        return piece(c, k, x) + back_in[c, k].astype(F32) + fwd_in[c, k].astype(F32)
+
+    def gcopy(c, j, k):
+        ahead, behind = x_ends(c, k)
+        slot = (x, x, x, behind, behind, ahead, x_opp)[j]
         to = (
             {"dp": 2 * ahead + core}, {"dp": 2 * behind + core}, peer,
             {"dp": 2 * ahead + core}, peer, peer, peer,
-        )[k]
-        return pltpu.make_async_remote_copy(
-            src_ref=act.at[c, core, slot], dst_ref=act.at[c, core, slot],
-            send_sem=g_send.at[c, k], recv_sem=g_recv.at[c, k],
+        )[j]
+        return pltpu.make_async_remote_copy(
+            src_ref=act.at[c, k, core, slot], dst_ref=act.at[c, k, core, slot],
+            send_sem=g_send.at[c, k, j], recv_sem=g_recv.at[c, k, j],
             device_id=to, device_id_type=MESH,
         )
 
-    def x_third(c):
-        sums = []
-        for k in range(3):
-            xcopy(c, 1, k).wait_recv()
-            xcopy(c, 2, k).wait_recv()
-            sums.append(
-                piece(c, k, x) + back_in[c, k].astype(F32) + fwd_in[c, k].astype(F32)
-            )
-        pre_gate, pre_up, hid_grad = sums
+    def spread(c, k):
+        for j in (0, 1, 2):
+            gcopy(c, j, k).start()
+
+    def forward(c):
+        pre_gate, pre_up = x_sum(c, 0), x_sum(c, 1)
+        gu[c, 0] = pre_gate
+        gu[c, 1] = pre_up
+        act[c, 0, core, x] = (pre_gate * jax.nn.sigmoid(pre_gate) * pre_up).astype(BF16)
+        spread(c, 0)
+
+    def backward(c):
+        hid_grad = x_sum(c, 2)
+        pre_gate, pre_up = gu[c, 0], gu[c, 1]
         squash = jax.nn.sigmoid(pre_gate)
-        act[c, core, x, :, :HALF] = (pre_gate * squash * pre_up).astype(BF16)
-        act[c, core, x, :, HALF:2 * HALF] = (
+        act[c, 1, core, x] = (
             hid_grad * pre_up * squash * (1.0 + pre_gate * (1.0 - squash))
         ).astype(BF16)
-        act[c, core, x, :, 2 * HALF:] = (hid_grad * pre_gate * squash).astype(BF16)
-        for k in (0, 1, 2):
-            gcopy(c, k).start()
-
-    def gather(c):
-        gcopy(c, 0).wait_recv()
-        gcopy(c, 3).start()
-        gcopy(c, 4).start()
-        gcopy(c, 1).wait_recv()
-        gcopy(c, 5).start()
-
-    def gather_end(c):
-        gcopy(c, 3).wait_recv()
-        gcopy(c, 6).start()
-        for k in (2, 4, 5, 6):
-            gcopy(c, k).wait_recv()
-
-    def rcopy(c, dy):
-        return pltpu.make_async_remote_copy(
-            src_ref=ret_out.at[c, mod(y + dy, NY)], dst_ref=ret_in.at[c, NY - dy],
-            send_sem=r_send.at[c, dy - 1], recv_sem=r_recv.at[c, dy - 1],
+        spread(c, 1)
+        act[c, 2, core, x] = (hid_grad * pre_gate * squash).astype(BF16)
+        spread(c, 2)
+
+    def gather(c, k):
+        gcopy(c, 0, k).wait_recv()
+        gcopy(c, 3, k).start()
+        gcopy(c, 4, k).start()
+        gcopy(c, 1, k).wait_recv()
+        gcopy(c, 5, k).start()
+
+    def gather_end(c, k):
+        gcopy(c, 3, k).wait_recv()
+        gcopy(c, 6, k).start()
+        for j in (2, 4, 5, 6):
+            gcopy(c, j, k).wait_recv()
+
+    def rcopy(c, dy, a):
+        return pltpu.make_async_remote_copy(
+            src_ref=ret_out.at[c, mod(y + dy, NY), a], dst_ref=ret_in.at[c, NY - dy, a],
+            send_sem=r_send.at[c, dy - 1, a], recv_sem=r_recv.at[c, dy - 1, a],
             device_id={"tp": mod(y + dy, NY)}, device_id_type=MESH,
         )
 
-    def results(c):
+    def results(c, a):
         at = slice(c * ROWS, (c + 1) * ROWS)
-        for k in range(3):
+        for k in ((0,), (1, 2))[a]:
             for h in (0, 1):
-                full[k, at, h * HALF:(h + 1) * HALF] = act[
-                    c, h, :, :, k * HALF:(k + 1) * HALF
-                ].reshape(ROWS, HALF)
-        eo = nt(full[0, at, :], wts[2]).astype(BF16)
-        ret_out[c, :, 0] = eo.reshape(NY, PIECE, WIDE)
-        rg = (nt(full[1, at, :], wts[0]) + nt(full[2, at, :], wts[1])).astype(BF16)
-        ret_out[c, :, 1] = rg.reshape(NY, PIECE, WIDE)
+                full[k, at, h * HALF:(h + 1) * HALF] = act[c, k, h].reshape(ROWS, HALF)
+        if a == 0:
+            value = nt(full[0, at, :], wts[2])
+        else:
+            value = nt(full[1, at, :], wts[0]) + nt(full[2, at, :], wts[1])
+        ret_out[c, :, a] = value.astype(BF16).reshape(NY, PIECE, WIDE)
         for dy in (2, 1, 3):
-            rcopy(c, dy).start()
-        ret_in[c, 0] = ret_out[c, y]
-
-    def combine(c):
+            rcopy(c, dy, a).start()
+        ret_in[c, 0, a] = ret_out[c, y, a]
+
+    def combine(c, a):
         for dy in range(1, NY):
-            rcopy(c, dy).wait_recv()
-        for a in (0, 1):
-            got = ret_in[c, :, a].reshape(ROWS, WIDE)
-            acc[a, 256 * c:256 * c + 256, :] = nn(cmat[c, a], got)
+            rcopy(c, dy, a).wait_recv()
+        got = ret_in[c, :, a].reshape(ROWS, WIDE)
+        acc[a, 256 * c:256 * c + 256, :] = nn(cmat[c, a], got)
 
     def weight_grad(k):
         lhs = xs[k // 2]
@@ -391,56 +390,111 @@
                     value = value + rs_in[a, way, e - 1].astype(F32)
         return value
 
-    flows = ((0, 0), (1, 1), (0, 1), (1, 0))
-
-    def send_sums(d):
-        for a, way in flows:
-            if d <= span(a, way):
-                rs_out[a, way, d - 1] = collected(a, way, d).astype(BF16)
-                scopy(a, way, d).start()
-
-    relay(2)
-    relay(4)
+    def send_sums(a, *ds):
+        for d in ds:
+            for way in RING:
+                if d <= span(a, way):
+                    rs_out[a, way, d - 1] = collected(a, way, d).astype(BF16)
+                    scopy(a, way, d).start()
+
+    relay(toks, 2)
+    relay(routes, 2)
+    relay(grds, 2)
+    relay(toks, 4)
+    relay(routes, 4)
+    relay(grds, 4)
     arrived(routes, 1, 4)
     route(0)
     pickers(0)
-    relay(6)
+    relay(toks, 6)
+    relay(routes, 6)
     for cp in own_copies:
         cp.wait()
-    arrived(values, 1, 4)
-    select(0)
+    arrived(toks, 1, 4)
+    select(0, 0)
+    relay(grds, 6)
+    arrived(grds, 1, 4)
+    select(0, 1)
     arrived(routes, 5, 8)
     route(1)
     pickers(1)
-    arrived(values, 5, 8)
-    select(1)
+    arrived(toks, 5, 8)
+    select(1, 0)
     for cp in w_copies:
         cp.wait()
-    partials(0)
+    partials(0, 0)
+    arrived(grds, 5, 8)
+    select(1, 1)
+    x_first(0, 0)
+    x_first(0, 1)
+    partials(0, 1)
+    x_first(0, 2)
+    partials(1, 0)
+    x_second(0, 0)
+    x_second(0, 1)
+    x_first(1, 0)
+    x_first(1, 1)
+    x_second(0, 2)
+    partials(1, 1)
+    x_first(1, 2)
+    forward(0)
+    x_second(1, 0)
+    x_second(1, 1)
+    backward(0)
+    x_second(1, 2)
+    gather(0, 0)
+    forward(1)
+    gather(0, 1)
+    gather(0, 2)
+    backward(1)
+    gather_end(0, 0)
+    gather(1, 0)
+    gather_end(0, 1)
+    gather_end(0, 2)
+    results(0, 0)
+    gather(1, 1)
+    gather(1, 2)
+    gather_end(1, 0)
+    results(1, 0)
+    results(0, 1)
     combiner(0)
-    x_first(0)
-    partials(1)
-    x_second(0)
-    x_first(1)
     combiner(1)
-    x_third(0)
-    x_second(1)
-    gather(0)
-    x_third(1)
-    gather_end(0)
-    results(0)
-    gather(1)
-    gather_end(1)
-    results(1)
+    gather_end(1, 1)
+    gather_end(1, 2)
+    results(1, 1)
+    combine(0, 0)
+    combine(1, 0)
+    send_sums(0, 8, 7)
+    combine(0, 1)
+    combine(1, 1)
+    send_sums(1, 8, 7)
+    weight_grad(2)
+    send_sums(0, 6, 5)
     weight_grad(0)
-    combine(0)
+    send_sums(1, 6, 5)
     weight_grad(1)
-    weight_grad(2)
-    combine(1)
-    send_sums(8)
-    send_sums(7)
-    for d in (6, 5, 4, 3, 2, 1):
-        send_sums(d)
+    send_sums(0, 4, 3)
+    send_sums(1, 4, 3)
+
+    for dy in range(1, NY):
+        my_copy(dy).wait_send()
+        for c in (0, 1):
+            for a in (0, 1):
+                ycopy(c, dy, a).wait_send()
+                rcopy(c, dy, a).wait_send()
+    send_sums(0, 2, 1)
+    send_sums(1, 2, 1)
+    for pair in routes + toks + grds:
+        for d in range(1, reach(*pair) + 1):
+            zcopy(*pair, d).wait_send()
+    for c in (0, 1):
+        for k in range(3):
+            core_copy(c, k).wait_send()
+            for kind in range(3):
+                xcopy(c, kind, k).wait_send()
+            for j in range(7):
+                gcopy(c, j, k).wait_send()
+
     for a, ref in ((0, lo_ref), (1, tg_ref)):
         value = acc[a, OWN * FOLD:(OWN + 1) * FOLD, :]
         for way in RING:
@@ -448,25 +502,10 @@
                 scopy(a, way, d).wait_recv()
                 value = value + rs_in[a, way, d - 1].astype(F32)
         ref[...] = value.astype(BF16)
-
-    for dy in range(1, NY):
-        my_copy(dy).wait_send()
-        for c in (0, 1):
-            ycopy(c, dy).wait_send()
-            rcopy(c, dy).wait_send()
-    for pair in routes + values:
-        for d in range(1, reach(*pair) + 1):
-            zcopy(*pair, d).wait_send()
-    for c in (0, 1):
-        for k in range(3):
-            core_copy(c, k).wait_send()
-            for kind in range(3):
-                xcopy(c, kind, k).wait_send()
-        for k in range(7):
-            gcopy(c, k).wait_send()
-    for a, way in flows:
-        for d in range(1, span(a, way) + 1):
-            scopy(a, way, d).wait_send()
+    for a in (0, 1):
+        for way in RING:
+            for d in range(1, span(a, way) + 1):
+                scopy(a, way, d).wait_send()
     for k in range(3):
         pltpu.make_async_copy(
             wgrad.at[k], (gg_hbm, ug_hbm, dg_hbm)[k].at[0], o_sem.at[k]
@@ -490,7 +529,6 @@
     vmem = pl.BlockSpec(memory_space=pltpu.VMEM)
     hbm = pl.BlockSpec(memory_space=pltpu.HBM)
     dma = pltpu.SemaphoreType.DMA
-    wide3 = 3 * HALF
     scratch = [
         pltpu.VMEM((2, NZ, BLOCK, FEAT), BF16),
         pltpu.VMEM((NY, 16, BLOCK), BF16),
@@ -508,7 +546,8 @@
         pltpu.VMEM((2, 3, ROWS, HALF), BF16),
         pltpu.VMEM((2, 3, ROWS, HALF), F32),
     ] + [pltpu.VMEM((2, 3, PIECE, HALF), BF16)] * 6 + [
-        pltpu.VMEM((2, 2, NX, PIECE, wide3), BF16),
+        pltpu.VMEM((2, 2, PIECE, HALF), F32),
+        pltpu.VMEM((2, 3, 2, NX, PIECE, HALF), BF16),
         pltpu.VMEM((3, 2 * ROWS, HID), BF16),
         pltpu.VMEM((2, NY, 2, PIECE, WIDE), BF16),
         pltpu.VMEM((2, NY, 2, PIECE, WIDE), BF16),
@@ -519,11 +558,11 @@
         pltpu.VMEM((3, WIDE, HID), BF16),
         dma((3, 2, 8)), dma((3, 2, 8)),
         dma((3,)), dma((3,)),
-        dma((2, 3)), dma((2, 3)),
+        dma((2, 3, 2)), dma((2, 3, 2)),
         dma((2, 3)), dma((2, 3)),
         dma((2, 3, 3)), dma((2, 3, 3)),
-        dma((2, 7)), dma((2, 7)),
-        dma((2, 3)), dma((2, 3)),
+        dma((2, 3, 7)), dma((2, 3, 7)),
+        dma((2, 3, 2)), dma((2, 3, 2)),
         dma((2, 2, 8)), dma((2, 2, 8)),
         dma((2,)), dma((3,)), dma((3,)),
     ]

time: 100 us -> 91.6 us (0.916)
  Pallas kernels: 98.3 us -> 89.7 us
    pallas_call x1, Pallas kernels: 95.6 us -> 87.1 us  [shards(): pl.pallas_call(body, out_shape=(fold, fold, weight, weight, weight), in_s...]
where the time goes in v3:
time: 91.6 us; the launch traced here: 90.4 us
  Pallas kernels  89.7 us (98%)
    pallas_call x1, Pallas kernels, shards(): pl.pallas_call(body, out_shape=(fold, fold, weight, weight, weight), in_s...  87.1 us
    pallas_call x1, Pallas kernels, shards(): pl.pallas_call(keep_body, out_shape=(fold, fold, weight, weight, weight),...  2.66 us

profile of v3, /device:TPU:6, one launch (start us, length us, event | category | flops | bytes accessed | tf_op | source)
XLA Modules:
  0.0 90.4 jit_solution(16467341840364258717)
XLA Ops:
  0.6 87.1 %shard_map.110 = (bf16[32,512]{1,0:T(8,128)(2,1)}, bf16[32,512]{1,0:T(8,128)(2,1)}, bf16[1,512,768]{2,1,0:T(8,128)(2,1)}, bf16[1,512,768]{2,1,0:T(8,128)(2,1)}, bf16[1,512,768]{2,1,0:T(8,128)(2,1)}) custom-call(s32[8,32]{1,0:T(8,128)} %bitcast.2, s32[8,32]{1,0:T(8,128)} %bitcast.3, bf16[128,128]{1,0:T(8,128)(2,1)} %tok_ref.1, bf16[128,128]{1,0:T(8,128)(2,1)} %grd_ref.1, ...), custom_call_target="tpu_custom_call" | custom-call | tf_op jit(solution)/shard_map/pallas_call | solution.py:572
  87.7 2.7 %shard_map.111 = (bf16[32,512]{1,0:T(8,128)(2,1)}, bf16[32,512]{1,0:T(8,128)(2,1)}, bf16[1,512,768]{2,1,0:T(8,128)(2,1)}, bf16[1,512,768]{2,1,0:T(8,128)(2,1)}, bf16[1,512,768]{2,1,0:T(8,128)(2,1)}) custom-call(bf16[32,512]{1,0:T(8,128)(2,1)} %get-tuple-element.10.refs_0_, bf16[32,512]{1,0:T(8,128)(2,1)} %get-tuple-element.11.refs_1_, ...), custom_call_target="tpu_custom_call" | custom-call | tf_op jit(solution)/shard_map/pallas_call | solution.py:584

commit v4 on v3

--- a/solution.py
+++ b/solution.py
@@ -437,7 +437,9 @@
     x_second(0, 2)
     partials(1, 1)
     x_first(1, 2)
+    combiner(0)
     forward(0)
+    combiner(1)
     x_second(1, 0)
     x_second(1, 1)
     backward(0)
@@ -457,8 +459,6 @@
     gather_end(1, 0)
     results(1, 0)
     results(0, 1)
-    combiner(0)
-    combiner(1)
     gather_end(1, 1)
     gather_end(1, 2)
     results(1, 1)
@@ -466,13 +466,13 @@
     combine(1, 0)
     send_sums(0, 8, 7)
     combine(0, 1)
+    weight_grad(2)
+    weight_grad(0)
+    weight_grad(1)
     combine(1, 1)
     send_sums(1, 8, 7)
-    weight_grad(2)
     send_sums(0, 6, 5)
-    weight_grad(0)
     send_sums(1, 6, 5)
-    weight_grad(1)
     send_sums(0, 4, 3)
     send_sums(1, 4, 3)
 
@@ -514,8 +514,16 @@
 
 def keep_body(*refs):
     sources, results, held, sems = refs[:5], refs[5:10], refs[10:15], refs[15]
-    into = [pltpu.make_async_copy(sources[i], held[i], sems.at[0, i]) for i in range(5)]
-    out = [pltpu.make_async_copy(held[i], results[i], sems.at[1, i]) for i in range(5)]
+    parts = [(0, pl.ds(0, FOLD)), (1, pl.ds(0, FOLD))]
+    parts += [(i, (0, pl.ds(h * 256, 256))) for i in (2, 3, 4) for h in (0, 1)]
+    into = [
+        pltpu.make_async_copy(sources[i].at[at], held[i].at[at], sems.at[0, n])
+        for n, (i, at) in enumerate(parts)
+    ]
+    out = [
+        pltpu.make_async_copy(held[i].at[at], results[i].at[at], sems.at[1, n])
+        for n, (i, at) in enumerate(parts)
+    ]
     for cp in into:
         cp.start()
     for first, second in zip(into, out):
@@ -587,7 +595,7 @@
         in_specs=hbm5,
         out_specs=hbm5,
         scratch_shapes=[pltpu.VMEM(out.shape, BF16) for out in (fold, fold, weight, weight, weight)]
-        + [dma((2, 5))],
+        + [dma((2, 8))],
     )(*results)
 
 

time: 91.6 us -> 91.7 us (level)
  no operation moved by 1% of the time
where the time goes in v4:
time: 91.7 us; the launch traced here: 90.2 us
  Pallas kernels  89.6 us (98%)
    pallas_call x1, Pallas kernels, shards(): pl.pallas_call(body, out_shape=(fold, fold, weight, weight, weight), in_s...  87 us
    pallas_call x1, Pallas kernels, shards(): pl.pallas_call(keep_body, out_shape=(fold, fold, weight, weight, weight),...  2.57 us

profile of v4, /device:TPU:6, one launch (start us, length us, event | category | flops | bytes accessed | tf_op | source)
XLA Modules:
  0.0 90.2 jit_solution(12271259308835812886)
XLA Ops:
  0.6 87.0 %shard_map.110 = (bf16[32,512]{1,0:T(8,128)(2,1)}, bf16[32,512]{1,0:T(8,128)(2,1)}, bf16[1,512,768]{2,1,0:T(8,128)(2,1)}, bf16[1,512,768]{2,1,0:T(8,128)(2,1)}, bf16[1,512,768]{2,1,0:T(8,128)(2,1)}) custom-call(s32[8,32]{1,0:T(8,128)} %bitcast.2, s32[8,32]{1,0:T(8,128)} %bitcast.3, bf16[128,128]{1,0:T(8,128)(2,1)} %tok_ref.1, bf16[128,128]{1,0:T(8,128)(2,1)} %grd_ref.1, ...), custom_call_target="tpu_custom_call" | custom-call | tf_op jit(solution)/shard_map/pallas_call | solution.py:580
  87.7 2.6 %shard_map.111 = (bf16[32,512]{1,0:T(8,128)(2,1)}, bf16[32,512]{1,0:T(8,128)(2,1)}, bf16[1,512,768]{2,1,0:T(8,128)(2,1)}, bf16[1,512,768]{2,1,0:T(8,128)(2,1)}, bf16[1,512,768]{2,1,0:T(8,128)(2,1)}) custom-call(bf16[32,512]{1,0:T(8,128)(2,1)} %get-tuple-element.10.refs_0_, bf16[32,512]{1,0:T(8,128)(2,1)} %get-tuple-element.11.refs_1_, ...), custom_call_target="tpu_custom_call" | custom-call | tf_op jit(solution)/shard_map/pallas_call | solution.py:592
